TPU v7x, 32 devices: a whole 2x2x4 slice. The times are simulated.
32 devices in a mesh: tm: 2 (over x), height: 16 (over z, y, core).
Axes of the slice: x: 2, y: 2, z: 4, core: 2. Of those that a mesh axis runs over, the one named last changes fastest.
Arguments:
- inputs: bfloat16 [4, 384, 4, 1024], P('tm', 'height'), may hold values from -24 to 24
- w_query: bfloat16 [1024, 1024], replicated, may hold values from -0.1875 to 0.1875
- w_key: bfloat16 [1024, 1024], replicated, may hold values from -0.1875 to 0.1875
- w_value: bfloat16 [1024, 1024], replicated, may hold values from -0.1875 to 0.1875
- w_out: bfloat16 [1024, 1024], replicated, may hold values from -0.1875 to 0.1875
- grad_out: bfloat16 [4, 384, 4, 1024], P('tm', 'height'), may hold values from -6 to 6
Outputs:
- attended: bfloat16 [4, 384, 4, 1024], P('tm', 'height')
- grad_in: bfloat16 [4, 384, 4, 1024], P('tm', 'height')
All inputs are finite; a program needn't handle non-finite values.
Results may differ from a plain program's by a relative error of at most 0.03.
The roundings to bfloat16 on the way count: a program that leaves them out, or rounds other values in their place, can miss the bound.
Values may be sent and summed in bfloat16 or wider, within the bound.
A program may use at most 128 MiB of HBM per device.

v0:
```python
import functools

import jax
import jax.numpy as jnp
from jax import lax
from jax.experimental import pallas as pl
from jax.experimental.pallas import tpu as pltpu
from jax.sharding import PartitionSpec as P

HD = 64
RT = 2
RH = 7
RW = 7
PAD = 8
BR = 8
NHG = 4
BF = jnp.bfloat16
F32 = jnp.float32


def dot_nn(a, b):
    return jnp.dot(a, b, preferred_element_type=F32)


def dot_nt(a, b):
    return lax.dot_general(a, b, (((1,), (1,)), ((), ())), preferred_element_type=F32)


def stack_heads(a):
    head = lax.broadcasted_iota(jnp.int32, a.shape, 1) // HD
    return jnp.concatenate([jnp.where(head == h, a, jnp.zeros_like(a)) for h in range(NHG)], axis=0)


def pick_heads(a):
    n = a.shape[0] // NHG
    head = lax.broadcasted_iota(jnp.int32, (n, a.shape[1]), 1) // HD
    out = a[:n]
    for h in range(1, NHG):
        out = jnp.where(head == h, a[h * n : (h + 1) * n], out)
    return out


def make_bias(block, dims):
    frames, rows, cols, slots, tm_size, height_size = dims
    t = lax.axis_index("tm")
    first = lax.axis_index("height") * rows
    span = (BR + 2 * PAD) * cols
    own = BR * cols
    shape = (frames * own, slots * span)
    i = lax.broadcasted_iota(jnp.int32, shape, 0)
    j = lax.broadcasted_iota(jnp.int32, shape, 1)
    qf = t * frames + i // own
    qr = (i % own) // cols
    slot = j // span
    kr = (j % span) // cols
    group = slot // frames
    if slots == 2 * frames:
        base = jnp.where(group == 0, t, 1 - t)
    else:
        base = jnp.where(group == 0, t, jnp.where(group == 1, t - 1, t + 1))
    kf = base * frames + slot % frames
    near = (jnp.abs(kf - qf) <= RT) & (jnp.abs(kr - PAD - qr) <= RH)
    row = first + block * BR + kr - PAD
    real = (kf >= 0) & (kf < tm_size * frames) & (row >= 0) & (row < height_size * rows)
    return jnp.where(near & real, 0.0, -1e30).astype(F32)


def forward_block(b, g, dims, q_ref, k_ref, v_ref, g_ref, mixed_ref, dq_ref, stat_ref, bias_ref):
    frames, rows, cols, slots, _, _ = dims
    own = BR * cols
    span = (BR + 2 * PAD) * cols
    width = NHG * HD
    at = pl.ds(g * width, width)
    mine = pl.ds(pl.multiple_of((b + 1) * own, own), own)
    inner = pl.ds(pl.multiple_of(b * own, own), own)
    wide = pl.ds(pl.multiple_of(b * own, own), span)
    q = stack_heads(q_ref[:frames, mine, at].reshape(frames * own, width))
    gr = stack_heads(g_ref[:frames, mine, at].reshape(frames * own, width))
    k = k_ref[:, wide, at].reshape(slots * span, width)
    v = v_ref[:, wide, at].reshape(slots * span, width)
    n = frames * own
    scale = HD ** (-0.5)
    s = dot_nt(q, k) * scale
    s = (s.reshape(NHG, n, slots * span) + bias_ref[...][None]).reshape(NHG * n, slots * span)
    top = jnp.max(s, axis=1, keepdims=True)
    e = jnp.exp(s - top)
    total = jnp.sum(e, axis=1, keepdims=True)
    p = e * (1.0 / total)
    mixed = dot_nn(p.astype(BF), v).astype(BF)
    delta = jnp.sum(gr.astype(F32) * mixed.astype(F32), axis=1, keepdims=True)
    dp = dot_nt(gr, v)
    ds = (p * ((dp - delta) * scale)).astype(BF)
    dq = dot_nn(ds, k)
    mixed_ref[:, inner, at] = pick_heads(mixed).reshape(frames, own, width)
    dq_ref[:, inner, at] = pick_heads(dq).astype(BF).reshape(frames, own, width)
    lse = top + jnp.log(total)
    lane = lax.broadcasted_iota(jnp.int32, (n, 128), 1)
    stat = stat_ref[:, inner, :].reshape(n, 128)
    for h in range(NHG):
        stat = jnp.where(lane == g * NHG + h, lse[h * n : (h + 1) * n], stat)
        stat = jnp.where(lane == 64 + g * NHG + h, delta[h * n : (h + 1) * n], stat)
    stat_ref[:, inner, :] = stat.reshape(frames, own, 128)


def backward_block(b, g, dims, q_ref, k_ref, v_ref, g_ref, dk_ref, dv_ref, flip_ref, bias_ref):
    frames, rows, cols, slots, _, _ = dims
    own = BR * cols
    span = (BR + 2 * PAD) * cols
    width = NHG * HD
    at = pl.ds(g * width, width)
    mine = pl.ds(pl.multiple_of((b + 1) * own, own), own)
    inner = pl.ds(pl.multiple_of(b * own, own), own)
    wide = pl.ds(pl.multiple_of(b * own, own), span)
    k = stack_heads(k_ref[:frames, mine, at].reshape(frames * own, width))
    v = stack_heads(v_ref[:frames, mine, at].reshape(frames * own, width))
    q = q_ref[:, wide, at].reshape(slots * span, width)
    gr = g_ref[:, wide, at].reshape(slots * span, width)
    n = frames * own
    full = (NHG, n, slots * span)
    scale = HD ** (-0.5)
    lse = flip_ref[g * NHG : (g + 1) * NHG, :]
    delta = flip_ref[64 + g * NHG : 64 + (g + 1) * NHG, :]
    s = dot_nt(k, q).reshape(full) * scale
    p = jnp.exp(s + bias_ref[...][None] - lse[:, None, :])
    dv = dot_nn(p.astype(BF).reshape(NHG * n, -1), gr)
    dp = dot_nt(v, gr).reshape(full)
    ds = (p * ((dp - delta[:, None, :]) * scale)).astype(BF)
    dk = dot_nn(ds.reshape(NHG * n, -1), q)
    dk_ref[:, inner, at] = pick_heads(dk).astype(BF).reshape(frames, own, width)
    dv_ref[:, inner, at] = pick_heads(dv).astype(BF).reshape(frames, own, width)


def project(src_ref, w_ref, dst_ref, slots, flip):
    width = w_ref.shape[0]
    tile = 256

    def tile_step(i, _):
        at = pl.ds(pl.multiple_of(i * tile, tile), tile)

        def slot_step(s, _):
            if flip:
                out = dot_nt(src_ref[s], w_ref[at, :])
            else:
                out = dot_nn(src_ref[s], w_ref[:, at])
            dst_ref[s, :, at] = out.astype(BF)
            return 0

        return lax.fori_loop(slots[0], slots[1], slot_step, 0)

    lax.fori_loop(0, width // tile, tile_step, 0)


def first_kernel(
    dims, x_ref, go_ref, wq_ref, wk_ref, wv_ref, wo_ref,
    attended_ref, dq_ref, stat_ref, k_ref, v_ref, q_ref, g_ref, mixed_ref, bias_ref,
):
    frames, rows, cols, slots, _, _ = dims
    project(x_ref, wq_ref, q_ref, (0, frames), False)
    project(go_ref, wo_ref, g_ref, (0, frames), True)
    project(x_ref, wk_ref, k_ref, (0, slots), False)
    project(x_ref, wv_ref, v_ref, (0, slots), False)
    stat_ref[...] = jnp.zeros_like(stat_ref)

    def step(b, _):
        bias_ref[...] = make_bias(b, dims)
        for g in range(x_ref.shape[2] // (NHG * HD)):
            forward_block(b, g, dims, q_ref, k_ref, v_ref, g_ref, mixed_ref, dq_ref, stat_ref, bias_ref)
        return 0

    lax.fori_loop(0, rows // BR, step, 0)
    project(mixed_ref, wo_ref, attended_ref, (0, frames), False)


def second_kernel(
    dims, x_ref, go_ref, wq_ref, wk_ref, wv_ref, wo_ref, k_ref, v_ref, dq_ref, stat_ref,
    out_ref, q_ref, g_ref, dk_ref, dv_ref, bias_ref, flip_ref,
):
    frames, rows, cols, slots, _, _ = dims
    own = BR * cols
    span = (BR + 2 * PAD) * cols
    project(x_ref, wq_ref, q_ref, (0, slots), False)
    project(go_ref, wo_ref, g_ref, (0, slots), True)

    def step(b, _):
        bias_ref[...] = make_bias(b, dims)
        stat = stat_ref[:, pl.ds(pl.multiple_of(b * own, own), span), :]
        flip_ref[...] = stat.reshape(slots * span, 128).T
        for g in range(x_ref.shape[2] // (NHG * HD)):
            backward_block(b, g, dims, q_ref, k_ref, v_ref, g_ref, dk_ref, dv_ref, flip_ref, bias_ref)
        return 0

    lax.fori_loop(0, rows // BR, step, 0)
    tile = 256

    def out_step(i, _):
        at = pl.ds(pl.multiple_of(i * tile, tile), tile)
        for f in range(frames):
            total = dot_nt(dq_ref[f], wq_ref[at, :])
            total += dot_nt(dk_ref[f], wk_ref[at, :])
            total += dot_nt(dv_ref[f], wv_ref[at, :])
            out_ref[f, :, at] = total.astype(BF)
        return 0

    lax.fori_loop(0, x_ref.shape[2] // tile, out_step, 0)


def around(block, edge):
    tm, height = lax.axis_size("tm"), lax.axis_size("height")
    if tm == 2:
        groups = [block, lax.ppermute(block, "tm", [(0, 1), (1, 0)])]
    else:
        up = [(i, i + 1) for i in range(tm - 1)]
        groups = [block, lax.ppermute(block, "tm", up), lax.ppermute(block, "tm", [(b, a) for a, b in up])]
    wide = jnp.concatenate(groups, axis=0)
    up = [(i, i + 1) for i in range(height - 1)]
    low = lax.ppermute(wide[:, -edge:], "height", up)
    high = lax.ppermute(wide[:, :edge], "height", [(b, a) for a, b in up])
    return jnp.concatenate([low, wide, high], axis=1)


def shards(inputs, w_query, w_key, w_value, w_out, grad_out):
    frames, rows, cols, width = inputs.shape
    tm, height = lax.axis_size("tm"), lax.axis_size("height")
    slots = (2 if tm == 2 else 3) * frames
    dims = (frames, rows, cols, slots, tm, height)
    edge = PAD * cols
    tokens = rows * cols
    wide = tokens + 2 * edge
    x = around(inputs.reshape(frames, tokens, width), edge)
    go = around(grad_out.reshape(frames, tokens, width), edge)
    keys = slots * (BR + 2 * PAD) * cols
    mine = frames * BR * cols
    params = pltpu.CompilerParams(vmem_limit_bytes=56 * 1024 * 1024)
    vmem = pl.BlockSpec(memory_space=pltpu.VMEM)
    attended, dq, stat, k, v = pl.pallas_call(
        functools.partial(first_kernel, dims),
        out_shape=[
            jax.ShapeDtypeStruct((frames, tokens, width), BF),
            jax.ShapeDtypeStruct((frames, tokens, width), BF),
            jax.ShapeDtypeStruct((frames, tokens, 128), F32),
            jax.ShapeDtypeStruct((slots, wide, width), BF),
            jax.ShapeDtypeStruct((slots, wide, width), BF),
        ],
        in_specs=[vmem] * 6,
        out_specs=[vmem] * 5,
        scratch_shapes=[
            pltpu.VMEM((frames, wide, width), BF),
            pltpu.VMEM((frames, wide, width), BF),
            pltpu.VMEM((frames, tokens, width), BF),
            pltpu.VMEM((mine, keys), F32),
        ],
        compiler_params=params,
        name="forward",
    )(x, go, w_query, w_key, w_value, w_out)
    stat = around(stat, edge)
    grad_in = pl.pallas_call(
        functools.partial(second_kernel, dims),
        out_shape=jax.ShapeDtypeStruct((frames, tokens, width), BF),
        in_specs=[vmem] * 10,
        out_specs=vmem,
        scratch_shapes=[
            pltpu.VMEM((slots, wide, width), BF),
            pltpu.VMEM((slots, wide, width), BF),
            pltpu.VMEM((frames, tokens, width), BF),
            pltpu.VMEM((frames, tokens, width), BF),
            pltpu.VMEM((mine, keys), F32),
            pltpu.VMEM((128, keys), F32),
        ],
        compiler_params=params,
        name="backward",
    )(x, go, w_query, w_key, w_value, w_out, k, v, dq, stat)
    shape = (frames, rows, cols, width)
    return attended.reshape(shape), grad_in.reshape(shape)


def solution(mesh):
    placed = (P("tm", "height", None, None), P(), P(), P(), P(), P("tm", "height", None, None))
    return jax.shard_map(
        shards,
        mesh=mesh,
        in_specs=placed,
        out_specs=(P("tm", "height", None, None), P("tm", "height", None, None)),
        check_vma=False,
    )
```

profile of v0, /device:TPU:7, one launch (start us, length us, event | category | flops | bytes accessed | tf_op | source)
XLA Modules:
  0.0 103.8 jit_solution(4135706281458673761)
XLA Ops:
  0.6 1.1 %reshape.17 = bf16[2,96,1024]{2,1,0:T(8,128)(2,1)S(1)} reshape(bf16[2,24,4,1024]{3,2,1,0:T(4,128)(2,1)} %param.11) | data formatting | bytes 786432 | tf_op jit(solution)/shard_map/reshape | solution.py:230
  1.7 0.3 collective-permute-start.3
  2.0 1.1 %reshape.16 = bf16[2,96,1024]{2,1,0:T(8,128)(2,1)S(1)} reshape(bf16[2,24,4,1024]{3,2,1,0:T(4,128)(2,1)} %param.6) | data formatting | bytes 786432 | tf_op jit(solution)/shard_map/reshape | solution.py:229
  3.1 1.3 %collective-permute-start = (bf16[2,96,1024]{2,1,0:T(8,128)(2,1)S(1)}, bf16[2,96,1024]{2,1,0:T(8,128)(2,1)S(1)}, u32[]{:S(2)}, u32[]{:S(2)}) collective-permute-start(bf16[2,96,1024]{2,1,0:T(8,128)(2,1)S(1)} %reshape.16), channel_id=1, source_target_pairs={{0,16},{16,0},{1,17},{17,1},{2,18},{18,2},{3,19},{19,3},{4,20},{20... | collective-permute-start | bytes 1179656 | tf_op jit(solution)/shard_map/ppermute | solution.py:210
  4.5 7.3 %collective-permute-done.3 = bf16[2,96,1024]{2,1,0:T(8,128)(2,1)S(1)} collective-permute-done((bf16[2,96,1024]{2,1,0:T(8,128)(2,1)S(1)}, bf16[2,96,1024]{2,1,0:T(8,128)(2,1)S(1)}, u32[]{:S(2)}, u32[]{:S(2)}) %collective-permute-start.3) | collective-permute-done | bytes 393248 | tf_op jit(solution)/shard_map/ppermute | solution.py:210
  11.8 5.7 %collective-permute-start.4 = (bf16[4,32,1024]{2,1,0:T(8,128)(2,1)S(1)}, bf16[4,32,1024]{2,1,0:T(8,128)(2,1)S(1)}, u32[]{:S(2)}, u32[]{:S(2)}) collective-permute-start(bf16[4,32,1024]{2,1,0:T(8,128)(2,1)S(1)} %get-tuple-element.12), channel_id=1, source_target_pairs={{0,1},{1,2},{2,3},{3,4},{4,5},{5,6},{6,7},{7,8},{8,9},{9,10},{10,1... | collective-permute-start | bytes 786440 | tf_op jit(solution)/shard_map/ppermute | solution.py:216
  17.6 1.9 %collective-permute-start.5 = (bf16[4,32,1024]{2,1,0:T(8,128)(2,1)S(1)}, bf16[4,32,1024]{2,1,0:T(8,128)(2,1)S(1)}, u32[]{:S(2)}, u32[]{:S(2)}) collective-permute-start(bf16[4,32,1024]{2,1,0:T(8,128)(2,1)S(1)} %get-tuple-element.13), channel_id=1, source_target_pairs={{1,0},{2,1},{3,2},{4,3},{5,4},{6,5},{7,6},{8,7},{9,8},{10,9},{11,1... | collective-permute-start | bytes 786440 | tf_op jit(solution)/shard_map/ppermute | solution.py:217
  19.5 0.7 collective-permute-done
  20.3 4.6 %collective-permute-start.1 = (bf16[4,32,1024]{2,1,0:T(8,128)(2,1)S(1)}, bf16[4,32,1024]{2,1,0:T(8,128)(2,1)S(1)}, u32[]{:S(2)}, u32[]{:S(2)}) collective-permute-start(bf16[4,32,1024]{2,1,0:T(8,128)(2,1)S(1)} %get-tuple-element.14), channel_id=1, source_target_pairs={{0,1},{1,2},{2,3},{3,4},{4,5},{5,6},{6,7},{7,8},{8,9},{9,10},{10,1... | collective-permute-start | bytes 786440 | tf_op jit(solution)/shard_map/ppermute | solution.py:216
  24.9 1.9 %collective-permute-start.2 = (bf16[4,32,1024]{2,1,0:T(8,128)(2,1)S(1)}, bf16[4,32,1024]{2,1,0:T(8,128)(2,1)S(1)}, u32[]{:S(2)}, u32[]{:S(2)}) collective-permute-start(bf16[4,32,1024]{2,1,0:T(8,128)(2,1)S(1)} %get-tuple-element.15), channel_id=1, source_target_pairs={{1,0},{2,1},{3,2},{4,3},{5,4},{6,5},{7,6},{8,7},{9,8},{10,9},{11,1... | collective-permute-start | bytes 786440 | tf_op jit(solution)/shard_map/ppermute | solution.py:217
  26.8 0.0 collective-permute-done.4
  26.8 0.0 collective-permute-done.5
  26.8 1.2 %pad_maximum_fusion.1.go_ref = bf16[4,160,1024]{2,1,0:T(8,128)(2,1)} fusion(bf16[4,32,1024]{2,1,0:T(8,128)(2,1)S(1)} %collective-permute-done.5, bf16[4,96,1024]{2,1,0:T(8,128)(2,1)S(1)} %constant_dynamic-update-slice_fusion.2, bf16[4,32,1024]{2,1,0:T(8,128)(2,1)S(1)} %collective-permute-done.4), kind=kLoop, calls=%fused_computation.1 | loop fusion | flops 3932160 | bytes 2621440 | tf_op jit(solution)/shard_map/concatenate | solution.py:218
  28.0 0.2 collective-permute-done.1
  28.2 5.3 %collective-permute-done.2 = bf16[4,32,1024]{2,1,0:T(8,128)(2,1)S(1)} collective-permute-done((bf16[4,32,1024]{2,1,0:T(8,128)(2,1)S(1)}, bf16[4,32,1024]{2,1,0:T(8,128)(2,1)S(1)}, u32[]{:S(2)}, u32[]{:S(2)}) %collective-permute-start.2) | collective-permute-done | bytes 262176 | tf_op jit(solution)/shard_map/ppermute | solution.py:217
  33.4 1.2 %pad_maximum_fusion.x_ref = bf16[4,160,1024]{2,1,0:T(8,128)(2,1)} fusion(bf16[4,32,1024]{2,1,0:T(8,128)(2,1)S(1)} %collective-permute-done.2, bf16[4,96,1024]{2,1,0:T(8,128)(2,1)S(1)} %constant_dynamic-update-slice_fusion, bf16[4,32,1024]{2,1,0:T(8,128)(2,1)S(1)} %collective-permute-done.1), kind=kLoop, calls=%fused_computation | loop fusion | flops 3932160 | bytes 2621440 | tf_op jit(solution)/shard_map/concatenate | solution.py:218
  34.6 28.6 %forward.1 = (bf16[2,96,1024]{2,1,0:T(8,128)(2,1)}, bf16[2,96,1024]{2,1,0:T(8,128)(2,1)}, f32[2,96,128]{2,1,0:T(8,128)}, bf16[4,160,1024]{2,1,0:T(8,128)(2,1)}, bf16[4,160,1024]{2,1,0:T(8,128)(2,1)}) custom-call(bf16[4,160,1024]{2,1,0:T(8,128)(2,1)} %pad_maximum_fusion.x_ref, bf16[4,160,1024]{2,1,0:T(8,128)(2,1)} %pad_maximum_fusion.1.go_ref, ...), custom_call_target="tpu_custom_call" | custom-call | tf_op jit(solution)/shard_map/forward/pallas_call | solution.py:235
  63.3 0.2 collective-permute-start.6
  63.5 0.9 constant_dynamic-update-slice_fusion.5
  64.4 2.5 %collective-permute-done.6 = f32[2,96,128]{2,1,0:T(8,128)S(1)} collective-permute-done((f32[2,96,128]{2,1,0:T(8,128)}, f32[2,96,128]{2,1,0:T(8,128)S(1)}, u32[]{:S(2)}, u32[]{:S(2)}) %collective-permute-start.6) | collective-permute-done | bytes 98336 | tf_op jit(solution)/shard_map/ppermute | solution.py:210
  67.0 3.9 %collective-permute-start.7 = (f32[4,32,128]{2,1,0:T(8,128)S(1)}, f32[4,32,128]{2,1,0:T(8,128)S(1)}, u32[]{:S(2)}, u32[]{:S(2)}) collective-permute-start(f32[4,32,128]{2,1,0:T(8,128)S(1)} %get-tuple-element.16), channel_id=1, source_target_pairs={{0,1},{1,2},{2,3},{3,4},{4,5},{5,6},{6,7},{7,8},{8,9},{9,10},{10,1... | collective-permute-start | bytes 196616 | tf_op jit(solution)/shard_map/ppermute | solution.py:216
  70.8 1.9 %collective-permute-start.8 = (f32[4,32,128]{2,1,0:T(8,128)S(1)}, f32[4,32,128]{2,1,0:T(8,128)S(1)}, u32[]{:S(2)}, u32[]{:S(2)}) collective-permute-start(f32[4,32,128]{2,1,0:T(8,128)S(1)} %get-tuple-element.17), channel_id=1, source_target_pairs={{1,0},{2,1},{3,2},{4,3},{5,4},{6,5},{7,6},{8,7},{9,8},{10,9},{11,1... | collective-permute-start | bytes 196616 | tf_op jit(solution)/shard_map/ppermute | solution.py:217
  72.8 1.9 %reshape.18 = bf16[2,24,4,1024]{3,2,1,0:T(4,128)(2,1)} reshape(bf16[2,96,1024]{2,1,0:T(8,128)(2,1)} %get-tuple-element.7) | data formatting | bytes 786432 | tf_op jit(solution)/shard_map/reshape | solution.py:273
  74.7 0.0 collective-permute-done.7
  74.7 2.7 %collective-permute-done.8 = f32[4,32,128]{2,1,0:T(8,128)S(1)} collective-permute-done((f32[4,32,128]{2,1,0:T(8,128)S(1)}, f32[4,32,128]{2,1,0:T(8,128)S(1)}, u32[]{:S(2)}, u32[]{:S(2)}) %collective-permute-start.8) | collective-permute-done | bytes 65568 | tf_op jit(solution)/shard_map/ppermute | solution.py:217
  77.3 0.7 pad_maximum_fusion.2.stat_ref
  78.1 23.8 %backward.1 = bf16[2,96,1024]{2,1,0:T(8,128)(2,1)} custom-call(bf16[4,160,1024]{2,1,0:T(8,128)(2,1)} %pad_maximum_fusion.x_ref, bf16[4,160,1024]{2,1,0:T(8,128)(2,1)} %pad_maximum_fusion.1.go_ref, bf16[1024,1024]{1,0:T(8,128)(2,1)} %wq_ref.3, bf16[1024,1024]{1,0:T(8,128)(2,1)} %wk_ref.3, bf16[1024,1024]{1,0:T(8,128)(2,1)} %wv_ref.3, ...), custom_call_target="tpu_custom_call" | custom-call | tf_op jit(solution)/shard_map/backward/pallas_call | solution.py:256
  101.9 1.9 %reshape.19 = bf16[2,24,4,1024]{3,2,1,0:T(4,128)(2,1)} reshape(bf16[2,96,1024]{2,1,0:T(8,128)(2,1)} %backward.1) | data formatting | bytes 786432 | tf_op jit(solution)/shard_map/reshape | solution.py:273
  (8 shorter events, 0.2 us)
Async XLA Ops:
  1.7 10.0 %collective-permute-start.3 = (bf16[2,96,1024]{2,1,0:T(8,128)(2,1)S(1)}, bf16[2,96,1024]{2,1,0:T(8,128)(2,1)S(1)}, u32[]{:S(2)}, u32[]{:S(2)}) collective-permute-start(bf16[2,96,1024]{2,1,0:T(8,128)(2,1)S(1)} %reshape.17), channel_id=1, source_target_pairs={{0,16},{16,0},{1,17},{17,1},{2,18},{18,2},{3,19},{19,3},{4,20},{20... | collective-permute-start | bytes 1179656 | tf_op jit(solution)/shard_map/ppermute | solution.py:210
  3.1 17.1 %collective-permute-start = (bf16[2,96,1024]{2,1,0:T(8,128)(2,1)S(1)}, bf16[2,96,1024]{2,1,0:T(8,128)(2,1)S(1)}, u32[]{:S(2)}, u32[]{:S(2)}) collective-permute-start(bf16[2,96,1024]{2,1,0:T(8,128)(2,1)S(1)} %reshape.16), channel_id=1, source_target_pairs={{0,16},{16,0},{1,17},{17,1},{2,18},{18,2},{3,19},{19,3},{4,20},{20... | collective-permute-start | bytes 1179656 | tf_op jit(solution)/shard_map/ppermute | solution.py:210
  11.8 14.9 %collective-permute-start.4 = (bf16[4,32,1024]{2,1,0:T(8,128)(2,1)S(1)}, bf16[4,32,1024]{2,1,0:T(8,128)(2,1)S(1)}, u32[]{:S(2)}, u32[]{:S(2)}) collective-permute-start(bf16[4,32,1024]{2,1,0:T(8,128)(2,1)S(1)} %get-tuple-element.12), channel_id=1, source_target_pairs={{0,1},{1,2},{2,3},{3,4},{4,5},{5,6},{6,7},{7,8},{8,9},{9,10},{10,1... | collective-permute-start | bytes 786440 | tf_op jit(solution)/shard_map/ppermute | solution.py:216
  17.6 9.2 %collective-permute-start.5 = (bf16[4,32,1024]{2,1,0:T(8,128)(2,1)S(1)}, bf16[4,32,1024]{2,1,0:T(8,128)(2,1)S(1)}, u32[]{:S(2)}, u32[]{:S(2)}) collective-permute-start(bf16[4,32,1024]{2,1,0:T(8,128)(2,1)S(1)} %get-tuple-element.13), channel_id=1, source_target_pairs={{1,0},{2,1},{3,2},{4,3},{5,4},{6,5},{7,6},{8,7},{9,8},{10,9},{11,1... | collective-permute-start | bytes 786440 | tf_op jit(solution)/shard_map/ppermute | solution.py:217
  20.3 7.9 %collective-permute-start.1 = (bf16[4,32,1024]{2,1,0:T(8,128)(2,1)S(1)}, bf16[4,32,1024]{2,1,0:T(8,128)(2,1)S(1)}, u32[]{:S(2)}, u32[]{:S(2)}) collective-permute-start(bf16[4,32,1024]{2,1,0:T(8,128)(2,1)S(1)} %get-tuple-element.14), channel_id=1, source_target_pairs={{0,1},{1,2},{2,3},{3,4},{4,5},{5,6},{6,7},{7,8},{8,9},{9,10},{10,1... | collective-permute-start | bytes 786440 | tf_op jit(solution)/shard_map/ppermute | solution.py:216
  24.9 8.6 %collective-permute-start.2 = (bf16[4,32,1024]{2,1,0:T(8,128)(2,1)S(1)}, bf16[4,32,1024]{2,1,0:T(8,128)(2,1)S(1)}, u32[]{:S(2)}, u32[]{:S(2)}) collective-permute-start(bf16[4,32,1024]{2,1,0:T(8,128)(2,1)S(1)} %get-tuple-element.15), channel_id=1, source_target_pairs={{1,0},{2,1},{3,2},{4,3},{5,4},{6,5},{7,6},{8,7},{9,8},{10,9},{11,1... | collective-permute-start | bytes 786440 | tf_op jit(solution)/shard_map/ppermute | solution.py:217
  63.3 3.7 %collective-permute-start.6 = (f32[2,96,128]{2,1,0:T(8,128)}, f32[2,96,128]{2,1,0:T(8,128)S(1)}, u32[]{:S(2)}, u32[]{:S(2)}) collective-permute-start(f32[2,96,128]{2,1,0:T(8,128)} %get-tuple-element.11), channel_id=1, source_target_pairs={{0,16},{16,0},{1,17},{17,1},{2,18},{18,2},{3,19},{19,3},{4,20},{20... | collective-permute-start | bytes 294920 | tf_op jit(solution)/shard_map/ppermute | solution.py:210
  67.0 7.7 %collective-permute-start.7 = (f32[4,32,128]{2,1,0:T(8,128)S(1)}, f32[4,32,128]{2,1,0:T(8,128)S(1)}, u32[]{:S(2)}, u32[]{:S(2)}) collective-permute-start(f32[4,32,128]{2,1,0:T(8,128)S(1)} %get-tuple-element.16), channel_id=1, source_target_pairs={{0,1},{1,2},{2,3},{3,4},{4,5},{5,6},{6,7},{7,8},{8,9},{9,10},{10,1... | collective-permute-start | bytes 196616 | tf_op jit(solution)/shard_map/ppermute | solution.py:216
  70.8 6.5 %collective-permute-start.8 = (f32[4,32,128]{2,1,0:T(8,128)S(1)}, f32[4,32,128]{2,1,0:T(8,128)S(1)}, u32[]{:S(2)}, u32[]{:S(2)}) collective-permute-start(f32[4,32,128]{2,1,0:T(8,128)S(1)} %get-tuple-element.17), channel_id=1, source_target_pairs={{1,0},{2,1},{3,2},{4,3},{5,4},{6,5},{7,6},{8,7},{9,8},{10,9},{11,1... | collective-permute-start | bytes 196616 | tf_op jit(solution)/shard_map/ppermute | solution.py:217
where the time goes:
time: 104 us
  Pallas kernels  52.5 us (50%)
  starting transfers between devices  21.8 us (21%)
  waiting for transfers between devices  18.6 us (18%)
  local copies, waits for them, and re-layouts  7.08 us (7%)
  other arithmetic  3.08 us (3%)
    pallas_call x1, Pallas kernels, shards(): pl.pallas_call(functools.partial(first_kernel, dims), out_shape=[jax.Shap...  28.6 us
    pallas_call x1, Pallas kernels, shards(): pl.pallas_call(functools.partial(second_kernel, dims), out_shape=jax.Shap...  23.8 us
    ppermute x3, starting transfers between devices, around(): low = lax.ppermute(wide[:, -edge:], 'height', up)  14.2 us
    ppermute x3, waiting for transfers between devices, around(): groups = [block, lax.ppermute(block, 'tm', [(0, 1), (1, 0)])]  10.5 us
    ppermute x3, waiting for transfers between devices, around(): high = lax.ppermute(wide[:, :edge], 'height', [(b, a) for a, b in up])  7.96 us
    ppermute x3, starting transfers between devices, around(): high = lax.ppermute(wide[:, :edge], 'height', [(b, a) for a, b in up])  5.76 us
    reshape x2, local copies, waits for them, and re-layouts, shards(): return (attended.reshape(shape), grad_in.reshape(shape))  3.78 us
    concatenate x3, other arithmetic, around(): return jnp.concatenate([low, wide, high], axis=1)  3.08 us
  transfers between devices with their start and end apart: 9, of which 6 were waited for; matrix products, arithmetic and copies ran while one was open for 5% of the time, Pallas kernels for 0%

commit v1 on v0

v1 whole, which is shorter than its diff:
```python
import functools

import jax
import jax.numpy as jnp
from jax import lax
from jax.experimental import pallas as pl
from jax.experimental.pallas import tpu as pltpu
from jax.sharding import PartitionSpec as P

HD = 64
RT = 2
RH = 7
RW = 7
PAD = 8
BR = 8
NHG = 4
BF = jnp.bfloat16
F32 = jnp.float32


def dot_nn(a, b):
    return jnp.dot(a, b, preferred_element_type=F32)


def dot_nt(a, b):
    return lax.dot_general(a, b, (((1,), (1,)), ((), ())), preferred_element_type=F32)


def stack_heads(a):
    head = lax.broadcasted_iota(jnp.int32, a.shape, 1) // HD
    return jnp.concatenate([jnp.where(head == h, a, jnp.zeros_like(a)) for h in range(NHG)], axis=0)


def pick_heads(a):
    n = a.shape[0] // NHG
    head = lax.broadcasted_iota(jnp.int32, (n, a.shape[1]), 1) // HD
    out = a[:n]
    for h in range(1, NHG):
        out = jnp.where(head == h, a[h * n : (h + 1) * n], out)
    return out


def make_bias(block, dims):
    frames, rows, cols, slots, tm_size, height_size = dims
    t = lax.axis_index("tm")
    first = lax.axis_index("height") * rows
    span = (BR + 2 * PAD) * cols
    own = BR * cols
    shape = (frames * own, slots * span)
    i = lax.broadcasted_iota(jnp.int32, shape, 0)
    j = lax.broadcasted_iota(jnp.int32, shape, 1)
    qf = t * frames + i // own
    qr = (i % own) // cols
    slot = j // span
    kr = (j % span) // cols
    group = slot // frames
    if slots == 2 * frames:
        base = jnp.where(group == 0, t, 1 - t)
    else:
        base = jnp.where(group == 0, t, jnp.where(group == 1, t - 1, t + 1))
    kf = base * frames + slot % frames
    near = (jnp.abs(kf - qf) <= RT) & (jnp.abs(kr - PAD - qr) <= RH)
    row = first + block * BR + kr - PAD
    real = (kf >= 0) & (kf < tm_size * frames) & (row >= 0) & (row < height_size * rows)
    return jnp.where(near & real, 0.0, -1e30).astype(F32)


def forward_block(b, g, dims, q_ref, k_ref, v_ref, g_ref, mixed_ref, dq_ref, stat, bias):
    frames, rows, cols, slots, _, _ = dims
    own = BR * cols
    span = (BR + 2 * PAD) * cols
    width = NHG * HD
    at = pl.ds(g * width, width)
    mine = pl.ds(pl.multiple_of((b + 1) * own, own), own)
    inner = pl.ds(pl.multiple_of(b * own, own), own)
    wide = pl.ds(pl.multiple_of(b * own, own), span)
    q = stack_heads(q_ref[:frames, mine, at].reshape(frames * own, width))
    gr = stack_heads(g_ref[:frames, mine, at].reshape(frames * own, width))
    k = k_ref[:, wide, at].reshape(slots * span, width)
    v = v_ref[:, wide, at].reshape(slots * span, width)
    n = frames * own
    s = dot_nt(q, k)
    s = (s.reshape(NHG, n, slots * span) + bias[None]).reshape(NHG * n, slots * span)
    top = jnp.max(s, axis=1, keepdims=True)
    e = jnp.exp(s - top)
    total = jnp.sum(e, axis=1, keepdims=True)
    p = e * (1.0 / total)
    mixed = dot_nn(p.astype(BF), v).astype(BF)
    delta = jnp.sum(gr.astype(F32) * mixed.astype(F32), axis=1, keepdims=True)
    dp = dot_nt(gr, v)
    ds = (p * (dp - delta)).astype(BF)
    dq = dot_nn(ds, k)
    mixed_ref[:, inner, at] = pick_heads(mixed).reshape(frames, own, width)
    dq = pick_heads(dq) * HD ** (-0.5)
    dq_ref[:, inner, at] = dq.astype(BF).reshape(frames, own, width)
    lse = top + jnp.log(total)
    lane = lax.broadcasted_iota(jnp.int32, (n, 128), 1)
    for h in range(NHG):
        stat = jnp.where(lane == g * NHG + h, lse[h * n : (h + 1) * n], stat)
        stat = jnp.where(lane == 64 + g * NHG + h, delta[h * n : (h + 1) * n], stat)
    return stat


def backward_block(b, g, dims, q_ref, k_ref, v_ref, g_ref, dk_ref, dv_ref, flip, bias):
    frames, rows, cols, slots, _, _ = dims
    own = BR * cols
    span = (BR + 2 * PAD) * cols
    width = NHG * HD
    at = pl.ds(g * width, width)
    mine = pl.ds(pl.multiple_of((b + 1) * own, own), own)
    inner = pl.ds(pl.multiple_of(b * own, own), own)
    wide = pl.ds(pl.multiple_of(b * own, own), span)
    k = stack_heads(k_ref[:frames, mine, at].reshape(frames * own, width))
    v = stack_heads(v_ref[:frames, mine, at].reshape(frames * own, width))
    q = q_ref[:, wide, at].reshape(slots * span, width)
    gr = g_ref[:, wide, at].reshape(slots * span, width)
    n = frames * own
    full = (NHG, n, slots * span)
    lse = flip[g * NHG : (g + 1) * NHG, :]
    delta = flip[64 + g * NHG : 64 + (g + 1) * NHG, :]
    s = dot_nt(k, q).reshape(full)
    p = jnp.exp(s + bias[None] - lse[:, None, :])
    dv = dot_nn(p.astype(BF).reshape(NHG * n, -1), gr)
    dp = dot_nt(v, gr).reshape(full)
    ds = (p * (dp - delta[:, None, :])).astype(BF)
    dk = dot_nn(ds.reshape(NHG * n, -1), q)
    dk_ref[:, inner, at] = pick_heads(dk).astype(BF).reshape(frames, own, width)
    dv_ref[:, inner, at] = pick_heads(dv).astype(BF).reshape(frames, own, width)


def project(src_ref, jobs, slots, spans):
    width = src_ref.shape[2]
    tile = 256
    first, count = slots
    some = pl.ds(first, count)
    total = sum(size for _, size in spans)

    def step(i, _):
        at = pl.ds(pl.multiple_of(i * tile, tile), tile)
        parts = [src_ref[some, a : a + size, :].reshape(count * size, width) for a, size in spans]
        rows = parts[0] if len(parts) == 1 else jnp.concatenate(parts, axis=0)
        for w_ref, dst_ref, flip, factor in jobs:
            out = dot_nt(rows, w_ref[at, :]) if flip else dot_nn(rows, w_ref[:, at])
            out = out.astype(BF)
            if factor != 1:
                out = out * jnp.asarray(factor, BF)
            begin = 0
            for a, size in spans:
                piece = out[begin : begin + count * size]
                dst_ref[some, a : a + size, at] = piece.reshape(count, size, tile)
                begin += count * size
        return 0

    lax.fori_loop(0, width // tile, step, 0)


class Exchange:
    def __init__(self, ref, sems, dims, edge):
        frames, rows, cols, slots, tm, height = dims
        self.ref, self.edge, self.frames = ref, edge, frames
        self.t, self.h = lax.axis_index("tm"), lax.axis_index("height")
        self.tm, self.height = tm, height
        self.send_x, self.recv_x, self.send_h, self.recv_h = sems
        tokens = rows * cols
        self.pieces = [(edge, edge), (tokens, edge), (2 * edge, tokens - 2 * edge)]
        self.groups = slots // frames

    def links(self):
        if self.tm == 2:
            return [(1, 1 - self.t, None, None)]
        return [
            (1, self.t + 1, self.t < self.tm - 1, self.t > 0),
            (2, self.t - 1, self.t > 0, self.t < self.tm - 1),
        ]

    def tm_copy(self, link, piece):
        group, target, _, _ = self.links()[link]
        start, size = self.pieces[piece]
        rows = pl.ds(start, size)
        return pltpu.make_async_remote_copy(
            src_ref=self.ref.at[pl.ds(0, self.frames), rows],
            dst_ref=self.ref.at[pl.ds(group * self.frames, self.frames), rows],
            send_sem=self.send_x.at[link * 3 + piece],
            recv_sem=self.recv_x.at[link * 3 + piece],
            device_id=(target, self.h),
            device_id_type=pl.DeviceIdType.MESH,
        )

    def row_copy(self, group, up):
        low, high = self.pieces[0][0], self.pieces[1][0]
        end = high + self.edge
        some = pl.ds(group * self.frames, self.frames)
        src, dst = (high, 0) if up else (low, end)
        slot = group * 2 + int(up)
        return pltpu.make_async_remote_copy(
            src_ref=self.ref.at[some, pl.ds(src, self.edge)],
            dst_ref=self.ref.at[some, pl.ds(dst, self.edge)],
            send_sem=self.send_h.at[slot],
            recv_sem=self.recv_h.at[slot],
            device_id=(self.t, self.h + 1 if up else self.h - 1),
            device_id_type=pl.DeviceIdType.MESH,
        )

    def when(self, cond, act):
        if cond is None:
            act()
        else:
            pl.when(cond)(act)

    def clear(self):
        low, end = self.edge, self.pieces[1][0] + self.edge
        shape = self.ref.shape

        @pl.when(self.h == 0)
        def _():
            self.ref[:, 0:low, :] = jnp.zeros((shape[0], low, shape[2]), self.ref.dtype)

        @pl.when(self.h == self.height - 1)
        def _():
            self.ref[:, end:, :] = jnp.zeros((shape[0], low, shape[2]), self.ref.dtype)

        for group, _, _, there in self.links():
            if there is not None:

                @pl.when(jnp.logical_not(there))
                def _(group=group):
                    some = pl.ds(group * self.frames, self.frames)
                    self.ref[some, low:end, :] = jnp.zeros((self.frames, end - low, shape[2]), self.ref.dtype)

    def there(self, group):
        return None if group == 0 else self.links()[group - 1][3]

    def both(self, a, b):
        return b if a is None else a & b

    def send_tm(self):
        for piece in range(3):
            for link, (_, _, sends, _) in enumerate(self.links()):
                self.when(sends, lambda link=link, piece=piece: self.tm_copy(link, piece).start())

    def got_tm(self, pieces):
        for link, (_, _, _, gets) in enumerate(self.links()):
            for piece in pieces:
                self.when(gets, lambda link=link, piece=piece: self.tm_copy(link, piece).wait_recv())

    def send_rows(self, groups):
        for group in groups:
            there = self.there(group)
            self.when(self.both(there, self.h < self.height - 1), lambda g=group: self.row_copy(g, True).start())
            self.when(self.both(there, self.h > 0), lambda g=group: self.row_copy(g, False).start())

    def got_rows(self):
        for group in range(self.groups):
            there = self.there(group)
            self.when(self.both(there, self.h > 0), lambda g=group: self.row_copy(g, True).wait_recv())
            self.when(self.both(there, self.h < self.height - 1), lambda g=group: self.row_copy(g, False).wait_recv())

    def sent(self):
        for piece in range(3):
            for link, (_, _, sends, _) in enumerate(self.links()):
                self.when(sends, lambda link=link, piece=piece: self.tm_copy(link, piece).wait_send())
        for group in range(self.groups):
            there = self.there(group)
            self.when(self.both(there, self.h < self.height - 1), lambda g=group: self.row_copy(g, True).wait_send())
            self.when(self.both(there, self.h > 0), lambda g=group: self.row_copy(g, False).wait_send())


def meet(dims):
    _, _, _, _, tm, height = dims
    t, h = lax.axis_index("tm"), lax.axis_index("height")
    barrier = pltpu.get_barrier_semaphore()
    count = jnp.int32(0)
    others = [(h > 0, t, h - 1), (h < height - 1, t, h + 1)]
    if tm == 2:
        pl.semaphore_signal(barrier, inc=1, device_id=(1 - t, h), device_id_type=pl.DeviceIdType.MESH)
        count = count + 1
    else:
        others += [(t > 0, t - 1, h), (t < tm - 1, t + 1, h)]
    for cond, tt, hh in others:

        @pl.when(cond)
        def _(tt=tt, hh=hh):
            pl.semaphore_signal(barrier, inc=1, device_id=(tt, hh), device_id_type=pl.DeviceIdType.MESH)

        count = count + cond.astype(jnp.int32)
    pl.semaphore_wait(barrier, count)


def kernel(
    dims, x_hbm, go_hbm, wq_hbm, wk_hbm, wv_hbm, wo_hbm,
    attended_ref, out_ref,
    x_ref, go_ref, q_ref, k_ref, v_ref, g_ref, wq_ref, wk_ref, wv_ref, wo_ref,
    mixed_ref, dq_ref, dk_ref, dv_ref, stat_ref, bias_ref, local_sem,
    *sems,
):
    frames, rows, cols, slots, tm, height = dims
    width = x_ref.shape[2]
    own = BR * cols
    span = (BR + 2 * PAD) * cols
    edge = PAD * cols
    tokens = rows * cols
    blocks = rows // BR
    scale = HD ** (-0.5)
    mid = pl.ds(edge, tokens)
    loads = [
        pltpu.make_async_copy(x_hbm, x_ref.at[pl.ds(0, frames), mid], local_sem.at[0]),
        pltpu.make_async_copy(go_hbm, go_ref.at[pl.ds(0, frames), mid], local_sem.at[1]),
        pltpu.make_async_copy(wq_hbm, wq_ref, local_sem.at[2]),
        pltpu.make_async_copy(wk_hbm, wk_ref, local_sem.at[3]),
        pltpu.make_async_copy(wv_hbm, wv_ref, local_sem.at[4]),
        pltpu.make_async_copy(wo_hbm, wo_ref, local_sem.at[5]),
    ]
    for load in loads:
        load.start()
    ex_x = Exchange(x_ref, sems[0:4], dims, edge)
    ex_go = Exchange(go_ref, sems[4:8], dims, edge)
    ex_st = Exchange(stat_ref, sems[8:12], dims, edge)
    meet(dims)
    loads[0].wait()
    ex_x.send_tm()
    ex_x.send_rows([0])
    loads[1].wait()
    ex_go.send_tm()
    ex_go.send_rows([0])
    ex_x.clear()
    ex_go.clear()
    ex_st.clear()

    def fill(b, _):
        bias_ref[b] = make_bias(b, dims)
        return 0

    lax.fori_loop(0, blocks, fill, 0)
    centre = [(edge, tokens)]
    rims = [(0, edge), (edge + tokens, edge)]
    for load in loads[2:5]:
        load.wait()
    to_q = (wq_ref, q_ref, False, scale)
    to_k = (wk_ref, k_ref, False, 1)
    to_v = (wv_ref, v_ref, False, 1)
    to_g = (wo_ref, g_ref, True, 1)
    project(x_ref, [to_q, to_k, to_v], (0, frames), centre)
    loads[5].wait()
    project(go_ref, [to_g], (0, frames), centre)

    def forward(b):
        stat = jnp.zeros((frames * own, 128), F32)
        bias = bias_ref[b]
        for g in range(width // (NHG * HD)):
            stat = forward_block(b, g, dims, q_ref, k_ref, v_ref, g_ref, mixed_ref, dq_ref, stat, bias)
        at = pl.ds(pl.multiple_of((b + 1) * own, own), own)
        stat_ref[pl.ds(0, frames), at, :] = stat.reshape(frames, own, 128)

    def backward(b):
        at = pl.ds(pl.multiple_of(b * own, own), span)
        flip = stat_ref[:, at, :].reshape(slots * span, 128).T
        bias = bias_ref[b]
        for g in range(width // (NHG * HD)):
            backward_block(b, g, dims, q_ref, k_ref, v_ref, g_ref, dk_ref, dv_ref, flip, bias)

    def inner_blocks(act):
        def step(b, _):
            act(b)
            return 0

        lax.fori_loop(1, blocks - 1, step, 0)

    def outer_blocks(act):
        def step(i, _):
            act(i * (blocks - 1))
            return 0

        lax.fori_loop(0, 2, step, 0)

    others = list(range(1, slots // frames))
    ex_x.got_tm([0, 1])
    ex_x.send_rows(others)
    ex_x.got_tm([2])
    project(x_ref, [to_k, to_v], (frames, slots - frames), centre)
    inner_blocks(forward)
    ex_go.got_tm([0, 1])
    ex_go.send_rows(others)
    ex_x.got_rows()
    project(x_ref, [to_k, to_v], (0, slots), rims)
    outer_blocks(forward)
    ex_st.send_tm()
    ex_st.send_rows([0])
    project(mixed_ref, [(wo_ref, attended_ref, False, 1)], (0, frames), [(0, tokens)])
    ex_go.got_tm([2])
    ex_st.got_tm([0, 1])
    ex_st.send_rows(others)
    project(x_ref, [to_q], (frames, slots - frames), centre)
    project(go_ref, [to_g], (frames, slots - frames), centre)
    ex_st.got_tm([2])
    inner_blocks(backward)
    ex_go.got_rows()
    project(x_ref, [to_q], (0, slots), rims)
    project(go_ref, [to_g], (0, slots), rims)
    ex_st.got_rows()
    outer_blocks(backward)
    tile = 256

    def out_step(i, _):
        at = pl.ds(pl.multiple_of(i * tile, tile), tile)
        total = dot_nt(dq_ref[...].reshape(frames * tokens, width), wq_ref[at, :])
        total += dot_nt(dk_ref[...].reshape(frames * tokens, width), wk_ref[at, :])
        total += dot_nt(dv_ref[...].reshape(frames * tokens, width), wv_ref[at, :])
        out_ref[:, :, at] = total.astype(BF).reshape(frames, tokens, tile)
        return 0

    lax.fori_loop(0, width // tile, out_step, 0)
    ex_x.sent()
    ex_go.sent()
    ex_st.sent()


def shards(inputs, w_query, w_key, w_value, w_out, grad_out):
    frames, rows, cols, width = inputs.shape
    tm, height = lax.axis_size("tm"), lax.axis_size("height")
    groups = 2 if tm == 2 else 3
    slots = groups * frames
    dims = (frames, rows, cols, slots, tm, height)
    tokens = rows * cols
    wide = tokens + 2 * PAD * cols
    keys = slots * (BR + 2 * PAD) * cols
    mine = frames * BR * cols
    vmem = pl.BlockSpec(memory_space=pltpu.VMEM)
    hbm = pl.BlockSpec(memory_space=pl.ANY)
    links = 3 * (groups - 1)
    sems = [pltpu.SemaphoreType.DMA((links,))] * 2 + [pltpu.SemaphoreType.DMA((2 * groups,))] * 2
    attended, grad_in = pl.pallas_call(
        functools.partial(kernel, dims),
        out_shape=[jax.ShapeDtypeStruct((frames, tokens, width), BF)] * 2,
        in_specs=[hbm] * 6,
        out_specs=[vmem] * 2,
        scratch_shapes=[pltpu.VMEM((slots, wide, width), BF)] * 6
        + [pltpu.VMEM((width, width), BF)] * 4
        + [pltpu.VMEM((frames, tokens, width), BF)] * 4
        + [
            pltpu.VMEM((slots, wide, 128), F32),
            pltpu.VMEM((rows // BR, mine, keys), F32),
            pltpu.SemaphoreType.DMA((6,)),
        ]
        + sems * 3,
        compiler_params=pltpu.CompilerParams(
            vmem_limit_bytes=56 * 1024 * 1024, collective_id=0, has_side_effects=True
        ),
        name="attention",
    )(
        inputs.reshape(frames, tokens, width), grad_out.reshape(frames, tokens, width),
        w_query, w_key, w_value, w_out,
    )
    shape = (frames, rows, cols, width)
    return attended.reshape(shape), grad_in.reshape(shape)


def solution(mesh):
    placed = (P("tm", "height", None, None), P(), P(), P(), P(), P("tm", "height", None, None))
    return jax.shard_map(
        shards,
        mesh=mesh,
        in_specs=placed,
        out_specs=(P("tm", "height", None, None), P("tm", "height", None, None)),
        check_vma=False,
    )
```

time: 104 us -> 51 us (0.49)
  the two profiles are of different devices: /device:TPU:7 before, /device:TPU:0 now
where the time goes in v1:
time: 51 us; the launch traced here: 50.7 us
  Pallas kernels  42.7 us (84%)
  local copies, waits for them, and re-layouts  7.44 us (15%)
  between operations  0.64 us (1%)
    pallas_call x1, Pallas kernels, shards(): pl.pallas_call(functools.partial(kernel, dims), out_shape=[jax.ShapeDtype...  42.7 us
    reshape x2, local copies, waits for them, and re-layouts, shards(): return (attended.reshape(shape), grad_in.reshape(shape))  3.78 us
    reshape x1, local copies, waits for them, and re-layouts, shards(): inputs.reshape(frames, tokens, width)  1.83 us
    reshape x1, local copies, waits for them, and re-layouts, shards(): grad_out.reshape(frames, tokens, width)  1.83 us

profile of v1, /device:TPU:0, one launch (start us, length us, event | category | flops | bytes accessed | tf_op | source)
XLA Modules:
  0.0 50.7 jit_solution(16655432448170506259)
XLA Ops:
  0.6 1.8 %reshape.16.x_hbm = bf16[2,96,1024]{2,1,0:T(8,128)(2,1)} reshape(bf16[2,24,4,1024]{3,2,1,0:T(4,128)(2,1)} %param.6) | data formatting | bytes 786432 | tf_op jit(solution)/shard_map/reshape | solution.py:450
  2.5 1.8 %reshape.17.go_hbm = bf16[2,96,1024]{2,1,0:T(8,128)(2,1)} reshape(bf16[2,24,4,1024]{3,2,1,0:T(4,128)(2,1)} %param.11) | data formatting | bytes 786432 | tf_op jit(solution)/shard_map/reshape | solution.py:450
  4.3 42.7 %attention.1 = (bf16[2,96,1024]{2,1,0:T(8,128)(2,1)}, bf16[2,96,1024]{2,1,0:T(8,128)(2,1)}) custom-call(bf16[2,96,1024]{2,1,0:T(8,128)(2,1)} %reshape.16.x_hbm, bf16[2,96,1024]{2,1,0:T(8,128)(2,1)} %reshape.17.go_hbm, bf16[1024,1024]{1,0:T(8,128)(2,1)} %wq_hbm.1, bf16[1024,1024]{1,0:T(8,128)(2,1)} %wk_hbm.1, bf16[1024,1024]{1,0:T(8,128)(2,1)} %wv_hbm.1, ...), custom_call_target="tpu_custom_call" | custom-call | tf_op jit(solution)/shard_map/attention/pallas_call | solution.py:431
  47.0 1.9 %reshape.18 = bf16[2,24,4,1024]{3,2,1,0:T(4,128)(2,1)} reshape(bf16[2,96,1024]{2,1,0:T(8,128)(2,1)} %get-tuple-element.4) | data formatting | bytes 786432 | tf_op jit(solution)/shard_map/reshape | solution.py:454
  48.8 1.9 %reshape.19 = bf16[2,24,4,1024]{3,2,1,0:T(4,128)(2,1)} reshape(bf16[2,96,1024]{2,1,0:T(8,128)(2,1)} %get-tuple-element.5) | data formatting | bytes 786432 | tf_op jit(solution)/shard_map/reshape | solution.py:454

commit v2 on v1

--- a/solution.py
+++ b/solution.py
@@ -147,7 +147,10 @@
             begin = 0
             for a, size in spans:
                 piece = out[begin : begin + count * size]
-                dst_ref[some, a : a + size, at] = piece.reshape(count, size, tile)
+                if len(dst_ref.shape) == 4:
+                    dst_ref[some, :, :, at] = piece.reshape(count, *dst_ref.shape[1:3], tile)
+                else:
+                    dst_ref[some, a : a + size, at] = piece.reshape(count, size, tile)
                 begin += count * size
         return 0
 
@@ -290,7 +293,7 @@
     dims, x_hbm, go_hbm, wq_hbm, wk_hbm, wv_hbm, wo_hbm,
     attended_ref, out_ref,
     x_ref, go_ref, q_ref, k_ref, v_ref, g_ref, wq_ref, wk_ref, wv_ref, wo_ref,
-    mixed_ref, dq_ref, dk_ref, dv_ref, stat_ref, bias_ref, local_sem,
+    mixed_ref, dq_ref, dk_ref, dv_ref, stat_ref, bias_ref, x4_ref, go4_ref, local_sem,
     *sems,
 ):
     frames, rows, cols, slots, tm, height = dims
@@ -303,8 +306,8 @@
     scale = HD ** (-0.5)
     mid = pl.ds(edge, tokens)
     loads = [
-        pltpu.make_async_copy(x_hbm, x_ref.at[pl.ds(0, frames), mid], local_sem.at[0]),
-        pltpu.make_async_copy(go_hbm, go_ref.at[pl.ds(0, frames), mid], local_sem.at[1]),
+        pltpu.make_async_copy(x_hbm, x4_ref, local_sem.at[0]),
+        pltpu.make_async_copy(go_hbm, go4_ref, local_sem.at[1]),
         pltpu.make_async_copy(wq_hbm, wq_ref, local_sem.at[2]),
         pltpu.make_async_copy(wk_hbm, wk_ref, local_sem.at[3]),
         pltpu.make_async_copy(wv_hbm, wv_ref, local_sem.at[4]),
@@ -315,11 +318,13 @@
     ex_x = Exchange(x_ref, sems[0:4], dims, edge)
     ex_go = Exchange(go_ref, sems[4:8], dims, edge)
     ex_st = Exchange(stat_ref, sems[8:12], dims, edge)
+    loads[0].wait()
+    x_ref[pl.ds(0, frames), mid, :] = x4_ref[...].reshape(frames, tokens, width)
     meet(dims)
-    loads[0].wait()
     ex_x.send_tm()
     ex_x.send_rows([0])
     loads[1].wait()
+    go_ref[pl.ds(0, frames), mid, :] = go4_ref[...].reshape(frames, tokens, width)
     ex_go.send_tm()
     ex_go.send_rows([0])
     ex_x.clear()
@@ -405,7 +410,7 @@
         total = dot_nt(dq_ref[...].reshape(frames * tokens, width), wq_ref[at, :])
         total += dot_nt(dk_ref[...].reshape(frames * tokens, width), wk_ref[at, :])
         total += dot_nt(dv_ref[...].reshape(frames * tokens, width), wv_ref[at, :])
-        out_ref[:, :, at] = total.astype(BF).reshape(frames, tokens, tile)
+        out_ref[:, :, :, at] = total.astype(BF).reshape(frames, rows, cols, tile)
         return 0
 
     lax.fori_loop(0, width // tile, out_step, 0)
@@ -428,9 +433,9 @@
     hbm = pl.BlockSpec(memory_space=pl.ANY)
     links = 3 * (groups - 1)
     sems = [pltpu.SemaphoreType.DMA((links,))] * 2 + [pltpu.SemaphoreType.DMA((2 * groups,))] * 2
-    attended, grad_in = pl.pallas_call(
+    return pl.pallas_call(
         functools.partial(kernel, dims),
-        out_shape=[jax.ShapeDtypeStruct((frames, tokens, width), BF)] * 2,
+        out_shape=[jax.ShapeDtypeStruct(inputs.shape, BF)] * 2,
         in_specs=[hbm] * 6,
         out_specs=[vmem] * 2,
         scratch_shapes=[pltpu.VMEM((slots, wide, width), BF)] * 6
@@ -439,6 +444,8 @@
         + [
             pltpu.VMEM((slots, wide, 128), F32),
             pltpu.VMEM((rows // BR, mine, keys), F32),
+            pltpu.VMEM(inputs.shape, BF),
+            pltpu.VMEM(inputs.shape, BF),
             pltpu.SemaphoreType.DMA((6,)),
         ]
         + sems * 3,
@@ -446,12 +453,7 @@
             vmem_limit_bytes=56 * 1024 * 1024, collective_id=0, has_side_effects=True
         ),
         name="attention",
-    )(
-        inputs.reshape(frames, tokens, width), grad_out.reshape(frames, tokens, width),
-        w_query, w_key, w_value, w_out,
-    )
-    shape = (frames, rows, cols, width)
-    return attended.reshape(shape), grad_in.reshape(shape)
+    )(inputs, grad_out, w_query, w_key, w_value, w_out)
 
 
 def solution(mesh):

time: 51 us -> 48.3 us (0.947)
  local copies, waits for them, and re-layouts: 7.44 us -> 3.76 us
  Pallas kernels: 42.7 us -> 43.7 us
    reshape x4 -> x0, local copies, waits for them, and re-layouts: 7.44 us -> none  [the longest x2 3.78 us: shards(): return (attended.reshape(shape), grad_in.reshape(shape))]
    unnamed x0 -> x2, local copies, waits for them, and re-layouts: none -> 3.76 us
    pallas_call x1, Pallas kernels: 42.7 us -> 43.7 us  [shards(): pl.pallas_call(functools.partial(kernel, dims), out_shape=[jax.ShapeDtype...]
where the time goes in v2:
time: 48.3 us; the launch traced here: 48.1 us
  Pallas kernels  43.7 us (90%)
  local copies, waits for them, and re-layouts  3.76 us (8%)
  between operations  0.64 us (1%)
    pallas_call x1, Pallas kernels, shards(): pl.pallas_call(functools.partial(kernel, dims), out_shape=[jax.ShapeDtype...  43.7 us
    unnamed x2, local copies, waits for them, and re-layouts  3.76 us

profile of v2, /device:TPU:0, one launch (start us, length us, event | category | flops | bytes accessed | tf_op | source)
XLA Modules:
  0.0 48.1 jit_solution(13477099506135509766)
XLA Ops:
  0.6 43.7 %attention.1 = (bf16[2,24,4,1024]{3,2,1,0:T(4,128)(2,1)}, bf16[2,24,4,1024]{3,2,1,0:T(4,128)(2,1)}) custom-call(bf16[2,24,4,1024]{3,2,1,0:T(4,128)(2,1)} %x_hbm.1, bf16[2,24,4,1024]{3,2,1,0:T(4,128)(2,1)} %go_hbm.1, bf16[1024,1024]{1,0:T(8,128)(2,1)} %wq_hbm.1, bf16[1024,1024]{1,0:T(8,128)(2,1)} %wk_hbm.1, bf16[1024,1024]{1,0:T(8,128)(2,1)} %wv_hbm.1, ...), custom_call_target="tpu_custom_call" | custom-call | tf_op jit(solution)/shard_map/attention/pallas_call | solution.py:436
  44.4 1.9 %copy.10 = bf16[2,24,4,1024]{3,2,1,0:T(4,128)(2,1)} copy(bf16[2,24,4,1024]{3,2,1,0:T(4,128)(2,1)} %get-tuple-element.4) | data formatting | bytes 786432
  46.2 1.9 %copy.11 = bf16[2,24,4,1024]{3,2,1,0:T(4,128)(2,1)} copy(bf16[2,24,4,1024]{3,2,1,0:T(4,128)(2,1)} %get-tuple-element.5) | data formatting | bytes 786432

commit v3 on v2

--- a/solution.py
+++ b/solution.py
@@ -65,67 +65,115 @@
     return jnp.where(near & real, 0.0, -1e30).astype(F32)
 
 
-def forward_block(b, g, dims, q_ref, k_ref, v_ref, g_ref, mixed_ref, dq_ref, stat, bias):
+def forward_rows(b, dims, q_ref, k_ref, v_ref, g_ref, mixed_ref, dq_ref, bias):
     frames, rows, cols, slots, _, _ = dims
     own = BR * cols
     span = (BR + 2 * PAD) * cols
     width = NHG * HD
-    at = pl.ds(g * width, width)
+    count = k_ref.shape[2] // width
+    n = frames * own
     mine = pl.ds(pl.multiple_of((b + 1) * own, own), own)
     inner = pl.ds(pl.multiple_of(b * own, own), own)
     wide = pl.ds(pl.multiple_of(b * own, own), span)
-    q = stack_heads(q_ref[:frames, mine, at].reshape(frames * own, width))
-    gr = stack_heads(g_ref[:frames, mine, at].reshape(frames * own, width))
-    k = k_ref[:, wide, at].reshape(slots * span, width)
-    v = v_ref[:, wide, at].reshape(slots * span, width)
-    n = frames * own
-    s = dot_nt(q, k)
-    s = (s.reshape(NHG, n, slots * span) + bias[None]).reshape(NHG * n, slots * span)
-    top = jnp.max(s, axis=1, keepdims=True)
-    e = jnp.exp(s - top)
-    total = jnp.sum(e, axis=1, keepdims=True)
-    p = e * (1.0 / total)
-    mixed = dot_nn(p.astype(BF), v).astype(BF)
-    delta = jnp.sum(gr.astype(F32) * mixed.astype(F32), axis=1, keepdims=True)
-    dp = dot_nt(gr, v)
-    ds = (p * (dp - delta)).astype(BF)
-    dq = dot_nn(ds, k)
-    mixed_ref[:, inner, at] = pick_heads(mixed).reshape(frames, own, width)
-    dq = pick_heads(dq) * HD ** (-0.5)
-    dq_ref[:, inner, at] = dq.astype(BF).reshape(frames, own, width)
-    lse = top + jnp.log(total)
-    lane = lax.broadcasted_iota(jnp.int32, (n, 128), 1)
-    for h in range(NHG):
-        stat = jnp.where(lane == g * NHG + h, lse[h * n : (h + 1) * n], stat)
-        stat = jnp.where(lane == 64 + g * NHG + h, delta[h * n : (h + 1) * n], stat)
-    return stat
-
-
-def backward_block(b, g, dims, q_ref, k_ref, v_ref, g_ref, dk_ref, dv_ref, flip, bias):
+    state = {}
+
+    def scores(g):
+        at = pl.ds(g * width, width)
+        q = stack_heads(q_ref[:frames, mine, at].reshape(n, width))
+        gr = stack_heads(g_ref[:frames, mine, at].reshape(n, width))
+        k = k_ref[:, wide, at].reshape(slots * span, width)
+        v = v_ref[:, wide, at].reshape(slots * span, width)
+        state[g] = [gr, dot_nt(q, k), dot_nt(gr, v)]
+
+    def soft(g):
+        s = state[g][1]
+        s = (s.reshape(NHG, n, slots * span) + bias[None]).reshape(NHG * n, slots * span)
+        top = jnp.max(s, axis=1, keepdims=True)
+        e = jnp.exp(s - top)
+        total = jnp.sum(e, axis=1, keepdims=True)
+        state[g] += [e * (1.0 / total), top + jnp.log(total)]
+
+    def mix(g):
+        at = pl.ds(g * width, width)
+        v = v_ref[:, wide, at].reshape(slots * span, width)
+        mixed = dot_nn(state[g][3].astype(BF), v).astype(BF)
+        state[g].append(mixed)
+        mixed_ref[:, inner, at] = pick_heads(mixed).reshape(frames, own, width)
+
+    def grads(g, stat):
+        at = pl.ds(g * width, width)
+        gr, _, dp, p, lse, mixed = state.pop(g)
+        delta = jnp.sum(gr.astype(F32) * mixed.astype(F32), axis=1, keepdims=True)
+        ds = (p * (dp - delta)).astype(BF)
+        k = k_ref[:, wide, at].reshape(slots * span, width)
+        dq = pick_heads(dot_nn(ds, k)) * HD ** (-0.5)
+        dq_ref[:, inner, at] = dq.astype(BF).reshape(frames, own, width)
+        lane = lax.broadcasted_iota(jnp.int32, (n, 128), 1)
+        for h in range(NHG):
+            stat = jnp.where(lane == g * NHG + h, lse[h * n : (h + 1) * n], stat)
+            stat = jnp.where(lane == 64 + g * NHG + h, delta[h * n : (h + 1) * n], stat)
+        return stat
+
+    stat = jnp.zeros((n, 128), F32)
+    scores(0)
+    scores(1)
+    soft(0)
+    for g in range(count):
+        if g + 2 < count:
+            scores(g + 2)
+        mix(g)
+        if g + 1 < count:
+            soft(g + 1)
+        stat = grads(g, stat)
+    return stat.reshape(frames, own, 128)
+
+
+def backward_rows(b, dims, q_ref, k_ref, v_ref, g_ref, dk_ref, dv_ref, flip, bias):
     frames, rows, cols, slots, _, _ = dims
     own = BR * cols
     span = (BR + 2 * PAD) * cols
     width = NHG * HD
-    at = pl.ds(g * width, width)
+    count = k_ref.shape[2] // width
+    n = frames * own
+    full = (NHG, n, slots * span)
     mine = pl.ds(pl.multiple_of((b + 1) * own, own), own)
     inner = pl.ds(pl.multiple_of(b * own, own), own)
     wide = pl.ds(pl.multiple_of(b * own, own), span)
-    k = stack_heads(k_ref[:frames, mine, at].reshape(frames * own, width))
-    v = stack_heads(v_ref[:frames, mine, at].reshape(frames * own, width))
-    q = q_ref[:, wide, at].reshape(slots * span, width)
-    gr = g_ref[:, wide, at].reshape(slots * span, width)
-    n = frames * own
-    full = (NHG, n, slots * span)
-    lse = flip[g * NHG : (g + 1) * NHG, :]
-    delta = flip[64 + g * NHG : 64 + (g + 1) * NHG, :]
-    s = dot_nt(k, q).reshape(full)
-    p = jnp.exp(s + bias[None] - lse[:, None, :])
-    dv = dot_nn(p.astype(BF).reshape(NHG * n, -1), gr)
-    dp = dot_nt(v, gr).reshape(full)
-    ds = (p * (dp - delta[:, None, :])).astype(BF)
-    dk = dot_nn(ds.reshape(NHG * n, -1), q)
-    dk_ref[:, inner, at] = pick_heads(dk).astype(BF).reshape(frames, own, width)
-    dv_ref[:, inner, at] = pick_heads(dv).astype(BF).reshape(frames, own, width)
+    state = {}
+
+    def scores(g):
+        at = pl.ds(g * width, width)
+        k = stack_heads(k_ref[:frames, mine, at].reshape(n, width))
+        v = stack_heads(v_ref[:frames, mine, at].reshape(n, width))
+        q = q_ref[:, wide, at].reshape(slots * span, width)
+        gr = g_ref[:, wide, at].reshape(slots * span, width)
+        state[g] = [dot_nt(k, q), dot_nt(v, gr)]
+
+    def soft(g):
+        s, dp = state[g]
+        lse = flip[g * NHG : (g + 1) * NHG, :]
+        delta = flip[64 + g * NHG : 64 + (g + 1) * NHG, :]
+        p = jnp.exp(s.reshape(full) + bias[None] - lse[:, None, :])
+        ds = p * (dp.reshape(full) - delta[:, None, :])
+        state[g] = [p.astype(BF).reshape(NHG * n, -1), ds.astype(BF).reshape(NHG * n, -1)]
+
+    def grads(g):
+        at = pl.ds(g * width, width)
+        p, ds = state.pop(g)
+        q = q_ref[:, wide, at].reshape(slots * span, width)
+        gr = g_ref[:, wide, at].reshape(slots * span, width)
+        dv_ref[:, inner, at] = pick_heads(dot_nn(p, gr)).astype(BF).reshape(frames, own, width)
+        dk_ref[:, inner, at] = pick_heads(dot_nn(ds, q)).astype(BF).reshape(frames, own, width)
+
+    scores(0)
+    scores(1)
+    soft(0)
+    for g in range(count):
+        if g + 2 < count:
+            scores(g + 2)
+        if g + 1 < count:
+            soft(g + 1)
+        grads(g)
 
 
 def project(src_ref, jobs, slots, spans):
@@ -252,8 +300,8 @@
             self.when(self.both(there, self.h < self.height - 1), lambda g=group: self.row_copy(g, True).start())
             self.when(self.both(there, self.h > 0), lambda g=group: self.row_copy(g, False).start())
 
-    def got_rows(self):
-        for group in range(self.groups):
+    def got_rows(self, groups):
+        for group in groups:
             there = self.there(group)
             self.when(self.both(there, self.h > 0), lambda g=group: self.row_copy(g, True).wait_recv())
             self.when(self.both(there, self.h < self.height - 1), lambda g=group: self.row_copy(g, False).wait_recv())
@@ -325,7 +373,6 @@
     ex_x.send_rows([0])
     loads[1].wait()
     go_ref[pl.ds(0, frames), mid, :] = go4_ref[...].reshape(frames, tokens, width)
-    ex_go.send_tm()
     ex_go.send_rows([0])
     ex_x.clear()
     ex_go.clear()
@@ -347,21 +394,20 @@
     project(x_ref, [to_q, to_k, to_v], (0, frames), centre)
     loads[5].wait()
     project(go_ref, [to_g], (0, frames), centre)
+    ex_x.got_rows([0])
+    project(x_ref, [to_q, to_k, to_v], (0, frames), rims)
+    ex_go.got_rows([0])
+    project(go_ref, [to_g], (0, frames), rims)
 
     def forward(b):
-        stat = jnp.zeros((frames * own, 128), F32)
-        bias = bias_ref[b]
-        for g in range(width // (NHG * HD)):
-            stat = forward_block(b, g, dims, q_ref, k_ref, v_ref, g_ref, mixed_ref, dq_ref, stat, bias)
+        stat = forward_rows(b, dims, q_ref, k_ref, v_ref, g_ref, mixed_ref, dq_ref, bias_ref[b])
         at = pl.ds(pl.multiple_of((b + 1) * own, own), own)
-        stat_ref[pl.ds(0, frames), at, :] = stat.reshape(frames, own, 128)
+        stat_ref[pl.ds(0, frames), at, :] = stat
 
     def backward(b):
         at = pl.ds(pl.multiple_of(b * own, own), span)
         flip = stat_ref[:, at, :].reshape(slots * span, 128).T
-        bias = bias_ref[b]
-        for g in range(width // (NHG * HD)):
-            backward_block(b, g, dims, q_ref, k_ref, v_ref, g_ref, dk_ref, dv_ref, flip, bias)
+        backward_rows(b, dims, q_ref, k_ref, v_ref, g_ref, dk_ref, dv_ref, flip, bias_ref[b])
 
     def inner_blocks(act):
         def step(b, _):
@@ -381,27 +427,26 @@
     ex_x.got_tm([0, 1])
     ex_x.send_rows(others)
     ex_x.got_tm([2])
-    project(x_ref, [to_k, to_v], (frames, slots - frames), centre)
+    ex_go.send_tm()
+    ex_x.got_rows(others)
+    rest = (frames, slots - frames)
+    project(x_ref, [to_k, to_v], rest, centre + rims)
     inner_blocks(forward)
     ex_go.got_tm([0, 1])
     ex_go.send_rows(others)
-    ex_x.got_rows()
-    project(x_ref, [to_k, to_v], (0, slots), rims)
     outer_blocks(forward)
     ex_st.send_tm()
     ex_st.send_rows([0])
     project(mixed_ref, [(wo_ref, attended_ref, False, 1)], (0, frames), [(0, tokens)])
     ex_go.got_tm([2])
+    project(x_ref, [to_q], rest, centre + rims)
     ex_st.got_tm([0, 1])
     ex_st.send_rows(others)
-    project(x_ref, [to_q], (frames, slots - frames), centre)
-    project(go_ref, [to_g], (frames, slots - frames), centre)
+    ex_go.got_rows(others)
+    project(go_ref, [to_g], rest, centre + rims)
     ex_st.got_tm([2])
     inner_blocks(backward)
-    ex_go.got_rows()
-    project(x_ref, [to_q], (0, slots), rims)
-    project(go_ref, [to_g], (0, slots), rims)
-    ex_st.got_rows()
+    ex_st.got_rows([0] + others)
     outer_blocks(backward)
     tile = 256
 
@@ -417,6 +462,20 @@
     ex_x.sent()
     ex_go.sent()
     ex_st.sent()
+
+
+def copy_kernel(a_hbm, b_hbm, a_out, b_out, sem):
+    copies = []
+    for i, (src, dst) in enumerate(((a_hbm, a_out), (b_hbm, b_out))):
+        parts = 4 * src.shape[0]
+        rows = src.shape[1] // 4
+        for part in range(parts):
+            at = (part // 4, pl.ds(part % 4 * rows, rows))
+            copies.append(pltpu.make_async_copy(src.at[at], dst.at[at], sem.at[i * parts + part]))
+    for copy in copies:
+        copy.start()
+    for copy in copies:
+        copy.wait()
 
 
 def shards(inputs, w_query, w_key, w_value, w_out, grad_out):
@@ -433,7 +492,7 @@
     hbm = pl.BlockSpec(memory_space=pl.ANY)
     links = 3 * (groups - 1)
     sems = [pltpu.SemaphoreType.DMA((links,))] * 2 + [pltpu.SemaphoreType.DMA((2 * groups,))] * 2
-    return pl.pallas_call(
+    both = pl.pallas_call(
         functools.partial(kernel, dims),
         out_shape=[jax.ShapeDtypeStruct(inputs.shape, BF)] * 2,
         in_specs=[hbm] * 6,
@@ -454,6 +513,14 @@
         ),
         name="attention",
     )(inputs, grad_out, w_query, w_key, w_value, w_out)
+    return pl.pallas_call(
+        copy_kernel,
+        out_shape=[jax.ShapeDtypeStruct(inputs.shape, BF)] * 2,
+        in_specs=[hbm] * 2,
+        out_specs=[hbm] * 2,
+        scratch_shapes=[pltpu.SemaphoreType.DMA((8 * frames,))],
+        name="copy_out",
+    )(*both)
 
 
 def solution(mesh):

time: 48.3 us -> 64.6 us (1.34)
  the two profiles are of different devices: /device:TPU:0 before, /device:TPU:1 now
where the time goes in v3:
time: 64.6 us; the launch traced here: 64.5 us
  Pallas kernels  63.8 us (99%)
    pallas_call x1, Pallas kernels, shards(): pl.pallas_call(functools.partial(kernel, dims), out_shape=[jax.ShapeDtype...  38.8 us
    pallas_call x1, Pallas kernels, shards(): pl.pallas_call(copy_kernel, out_shape=[jax.ShapeDtypeStruct(inputs.shape,...  25.1 us

profile of v3, /device:TPU:1, one launch (start us, length us, event | category | flops | bytes accessed | tf_op | source)
XLA Modules:
  0.0 64.5 jit_solution(17032397716353349889)
XLA Ops:
  0.6 38.8 %attention.1 = (bf16[2,24,4,1024]{3,2,1,0:T(4,128)(2,1)}, bf16[2,24,4,1024]{3,2,1,0:T(4,128)(2,1)}) custom-call(bf16[2,24,4,1024]{3,2,1,0:T(4,128)(2,1)} %x_hbm.1, bf16[2,24,4,1024]{3,2,1,0:T(4,128)(2,1)} %go_hbm.1, bf16[1024,1024]{1,0:T(8,128)(2,1)} %wq_hbm.1, bf16[1024,1024]{1,0:T(8,128)(2,1)} %wk_hbm.1, bf16[1024,1024]{1,0:T(8,128)(2,1)} %wv_hbm.1, ...), custom_call_target="tpu_custom_call" | custom-call | tf_op jit(solution)/shard_map/attention/pallas_call | solution.py:495
  39.4 25.1 %copy_out.1 = (bf16[2,24,4,1024]{3,2,1,0:T(4,128)(2,1)}, bf16[2,24,4,1024]{3,2,1,0:T(4,128)(2,1)}) custom-call(bf16[2,24,4,1024]{3,2,1,0:T(4,128)(2,1)} %get-tuple-element.4.a_hbm, bf16[2,24,4,1024]{3,2,1,0:T(4,128)(2,1)} %get-tuple-element.5.b_hbm), custom_call_target="tpu_custom_call" | custom-call | tf_op jit(solution)/shard_map/copy_out/pallas_call | solution.py:516

commit v4 on v3

--- a/solution.py
+++ b/solution.py
@@ -26,9 +26,8 @@
     return lax.dot_general(a, b, (((1,), (1,)), ((), ())), preferred_element_type=F32)
 
 
-def stack_heads(a):
-    head = lax.broadcasted_iota(jnp.int32, a.shape, 1) // HD
-    return jnp.concatenate([jnp.where(head == h, a, jnp.zeros_like(a)) for h in range(NHG)], axis=0)
+def stack_heads(a, mask_ref):
+    return (a[None] * mask_ref[...]).reshape(NHG * a.shape[0], a.shape[1])
 
 
 def pick_heads(a):
@@ -65,7 +64,7 @@
     return jnp.where(near & real, 0.0, -1e30).astype(F32)
 
 
-def forward_rows(b, dims, q_ref, k_ref, v_ref, g_ref, mixed_ref, dq_ref, bias):
+def forward_rows(b, dims, q_ref, k_ref, v_ref, g_ref, mixed_ref, dq_ref, bias, mask_ref):
     frames, rows, cols, slots, _, _ = dims
     own = BR * cols
     span = (BR + 2 * PAD) * cols
@@ -79,8 +78,8 @@
 
     def scores(g):
         at = pl.ds(g * width, width)
-        q = stack_heads(q_ref[:frames, mine, at].reshape(n, width))
-        gr = stack_heads(g_ref[:frames, mine, at].reshape(n, width))
+        q = stack_heads(q_ref[:frames, mine, at].reshape(n, width), mask_ref)
+        gr = stack_heads(g_ref[:frames, mine, at].reshape(n, width), mask_ref)
         k = k_ref[:, wide, at].reshape(slots * span, width)
         v = v_ref[:, wide, at].reshape(slots * span, width)
         state[g] = [gr, dot_nt(q, k), dot_nt(gr, v)]
@@ -128,7 +127,7 @@
     return stat.reshape(frames, own, 128)
 
 
-def backward_rows(b, dims, q_ref, k_ref, v_ref, g_ref, dk_ref, dv_ref, flip, bias):
+def backward_rows(b, dims, q_ref, k_ref, v_ref, g_ref, dk_ref, dv_ref, flip, bias, mask_ref):
     frames, rows, cols, slots, _, _ = dims
     own = BR * cols
     span = (BR + 2 * PAD) * cols
@@ -143,8 +142,8 @@
 
     def scores(g):
         at = pl.ds(g * width, width)
-        k = stack_heads(k_ref[:frames, mine, at].reshape(n, width))
-        v = stack_heads(v_ref[:frames, mine, at].reshape(n, width))
+        k = stack_heads(k_ref[:frames, mine, at].reshape(n, width), mask_ref)
+        v = stack_heads(v_ref[:frames, mine, at].reshape(n, width), mask_ref)
         q = q_ref[:, wide, at].reshape(slots * span, width)
         gr = g_ref[:, wide, at].reshape(slots * span, width)
         state[g] = [dot_nt(k, q), dot_nt(v, gr)]
@@ -176,18 +175,16 @@
         grads(g)
 
 
-def project(src_ref, jobs, slots, spans):
-    width = src_ref.shape[2]
+def project(jobs):
+    width = jobs[0][3].shape[0]
     tile = 256
-    first, count = slots
-    some = pl.ds(first, count)
-    total = sum(size for _, size in spans)
 
     def step(i, _):
         at = pl.ds(pl.multiple_of(i * tile, tile), tile)
-        parts = [src_ref[some, a : a + size, :].reshape(count * size, width) for a, size in spans]
-        rows = parts[0] if len(parts) == 1 else jnp.concatenate(parts, axis=0)
-        for w_ref, dst_ref, flip, factor in jobs:
+        for src_ref, (first, count), spans, w_ref, dst_ref, flip, factor in jobs:
+            some = pl.ds(first, count)
+            parts = [src_ref[some, a : a + size, :].reshape(count * size, width) for a, size in spans]
+            rows = parts[0] if len(parts) == 1 else jnp.concatenate(parts, axis=0)
             out = dot_nt(rows, w_ref[at, :]) if flip else dot_nn(rows, w_ref[:, at])
             out = out.astype(BF)
             if factor != 1:
@@ -316,7 +313,7 @@
             self.when(self.both(there, self.h > 0), lambda g=group: self.row_copy(g, False).wait_send())
 
 
-def meet(dims):
+def greet(dims):
     _, _, _, _, tm, height = dims
     t, h = lax.axis_index("tm"), lax.axis_index("height")
     barrier = pltpu.get_barrier_semaphore()
@@ -334,14 +331,14 @@
             pl.semaphore_signal(barrier, inc=1, device_id=(tt, hh), device_id_type=pl.DeviceIdType.MESH)
 
         count = count + cond.astype(jnp.int32)
-    pl.semaphore_wait(barrier, count)
+    return count
 
 
 def kernel(
     dims, x_hbm, go_hbm, wq_hbm, wk_hbm, wv_hbm, wo_hbm,
     attended_ref, out_ref,
     x_ref, go_ref, q_ref, k_ref, v_ref, g_ref, wq_ref, wk_ref, wv_ref, wo_ref,
-    mixed_ref, dq_ref, dk_ref, dv_ref, stat_ref, bias_ref, x4_ref, go4_ref, local_sem,
+    mixed_ref, dq_ref, dk_ref, dv_ref, stat_ref, bias_ref, x4_ref, go4_ref, mask_ref, local_sem,
     *sems,
 ):
     frames, rows, cols, slots, tm, height = dims
@@ -366,9 +363,10 @@
     ex_x = Exchange(x_ref, sems[0:4], dims, edge)
     ex_go = Exchange(go_ref, sems[4:8], dims, edge)
     ex_st = Exchange(stat_ref, sems[8:12], dims, edge)
+    count = greet(dims)
     loads[0].wait()
     x_ref[pl.ds(0, frames), mid, :] = x4_ref[...].reshape(frames, tokens, width)
-    meet(dims)
+    pl.semaphore_wait(pltpu.get_barrier_semaphore(), count)
     ex_x.send_tm()
     ex_x.send_rows([0])
     loads[1].wait()
@@ -383,31 +381,41 @@
         return 0
 
     lax.fori_loop(0, blocks, fill, 0)
+    head = lax.broadcasted_iota(jnp.int32, mask_ref.shape, 2) // HD
+    mask_ref[...] = (head == lax.broadcasted_iota(jnp.int32, mask_ref.shape, 0)).astype(F32).astype(BF)
     centre = [(edge, tokens)]
     rims = [(0, edge), (edge + tokens, edge)]
-    for load in loads[2:5]:
+    for load in loads[2:]:
         load.wait()
-    to_q = (wq_ref, q_ref, False, scale)
-    to_k = (wk_ref, k_ref, False, 1)
-    to_v = (wv_ref, v_ref, False, 1)
-    to_g = (wo_ref, g_ref, True, 1)
-    project(x_ref, [to_q, to_k, to_v], (0, frames), centre)
-    loads[5].wait()
-    project(go_ref, [to_g], (0, frames), centre)
+
+    def to_q(slots, spans):
+        return (x_ref, slots, spans, wq_ref, q_ref, False, scale)
+
+    def to_k(slots, spans):
+        return (x_ref, slots, spans, wk_ref, k_ref, False, 1)
+
+    def to_v(slots, spans):
+        return (x_ref, slots, spans, wv_ref, v_ref, False, 1)
+
+    def to_g(slots, spans):
+        return (go_ref, slots, spans, wo_ref, g_ref, True, 1)
+
+    first = (0, frames)
+    rest = (frames, slots - frames)
+    project([make(first, centre) for make in (to_q, to_k, to_v, to_g)])
     ex_x.got_rows([0])
-    project(x_ref, [to_q, to_k, to_v], (0, frames), rims)
     ex_go.got_rows([0])
-    project(go_ref, [to_g], (0, frames), rims)
+    project([make(first, rims) for make in (to_q, to_k, to_v, to_g)])
 
     def forward(b):
-        stat = forward_rows(b, dims, q_ref, k_ref, v_ref, g_ref, mixed_ref, dq_ref, bias_ref[b])
+        stat = forward_rows(b, dims, q_ref, k_ref, v_ref, g_ref, mixed_ref, dq_ref, bias_ref[b], mask_ref)
         at = pl.ds(pl.multiple_of((b + 1) * own, own), own)
         stat_ref[pl.ds(0, frames), at, :] = stat
 
     def backward(b):
         at = pl.ds(pl.multiple_of(b * own, own), span)
         flip = stat_ref[:, at, :].reshape(slots * span, 128).T
-        backward_rows(b, dims, q_ref, k_ref, v_ref, g_ref, dk_ref, dv_ref, flip, bias_ref[b])
+        backward_rows(b, dims, q_ref, k_ref, v_ref, g_ref, dk_ref, dv_ref, flip, bias_ref[b], mask_ref)
 
     def inner_blocks(act):
         def step(b, _):
@@ -429,21 +437,22 @@
     ex_x.got_tm([2])
     ex_go.send_tm()
     ex_x.got_rows(others)
-    rest = (frames, slots - frames)
-    project(x_ref, [to_k, to_v], rest, centre + rims)
+    project([to_k(rest, centre + rims), to_v(rest, centre + rims)])
     inner_blocks(forward)
     ex_go.got_tm([0, 1])
     ex_go.send_rows(others)
     outer_blocks(forward)
     ex_st.send_tm()
     ex_st.send_rows([0])
-    project(mixed_ref, [(wo_ref, attended_ref, False, 1)], (0, frames), [(0, tokens)])
     ex_go.got_tm([2])
-    project(x_ref, [to_q], rest, centre + rims)
+    ex_go.got_rows(others)
+    project([
+        to_q(rest, centre + rims),
+        to_g(rest, centre + rims),
+        (mixed_ref, first, [(0, tokens)], wo_ref, attended_ref, False, 1),
+    ])
     ex_st.got_tm([0, 1])
     ex_st.send_rows(others)
-    ex_go.got_rows(others)
-    project(go_ref, [to_g], rest, centre + rims)
     ex_st.got_tm([2])
     inner_blocks(backward)
     ex_st.got_rows([0] + others)
@@ -464,17 +473,19 @@
     ex_st.sent()
 
 
-def copy_kernel(a_hbm, b_hbm, a_out, b_out, sem):
-    copies = []
+def copy_kernel(a_hbm, b_hbm, a_out, b_out, held_ref, in_sem, out_sem):
+    arrive, leave = [], []
     for i, (src, dst) in enumerate(((a_hbm, a_out), (b_hbm, b_out))):
-        parts = 4 * src.shape[0]
-        rows = src.shape[1] // 4
-        for part in range(parts):
-            at = (part // 4, pl.ds(part % 4 * rows, rows))
-            copies.append(pltpu.make_async_copy(src.at[at], dst.at[at], sem.at[i * parts + part]))
-    for copy in copies:
+        for f in range(src.shape[0]):
+            slot = i * src.shape[0] + f
+            arrive.append(pltpu.make_async_copy(src.at[f], held_ref.at[slot], in_sem.at[slot]))
+            leave.append(pltpu.make_async_copy(held_ref.at[slot], dst.at[f], out_sem.at[slot]))
+    for copy in arrive:
         copy.start()
-    for copy in copies:
+    for before, after in zip(arrive, leave):
+        before.wait()
+        after.start()
+    for copy in leave:
         copy.wait()
 
 
@@ -505,6 +516,7 @@
             pltpu.VMEM((rows // BR, mine, keys), F32),
             pltpu.VMEM(inputs.shape, BF),
             pltpu.VMEM(inputs.shape, BF),
+            pltpu.VMEM((NHG, mine, NHG * HD), BF),
             pltpu.SemaphoreType.DMA((6,)),
         ]
         + sems * 3,
@@ -518,7 +530,11 @@
         out_shape=[jax.ShapeDtypeStruct(inputs.shape, BF)] * 2,
         in_specs=[hbm] * 2,
         out_specs=[hbm] * 2,
-        scratch_shapes=[pltpu.SemaphoreType.DMA((8 * frames,))],
+        scratch_shapes=[
+            pltpu.VMEM((2 * frames, rows, cols, width), BF),
+            pltpu.SemaphoreType.DMA((2 * frames,)),
+            pltpu.SemaphoreType.DMA((2 * frames,)),
+        ],
         name="copy_out",
     )(*both)
 

time: 64.6 us -> 41.2 us (0.64)
  Pallas kernels: 63.8 us -> 40.4 us
    pallas_call x1, Pallas kernels: 25.1 us -> 1.97 us  [shards(): pl.pallas_call(copy_kernel, out_shape=[jax.ShapeDtypeStruct(inputs.shape,...]
where the time goes in v4:
time: 41.2 us; the launch traced here: 41.1 us
  Pallas kernels  40.4 us (98%)
  between operations  0.64 us (2%)
    pallas_call x1, Pallas kernels, shards(): pl.pallas_call(functools.partial(kernel, dims), out_shape=[jax.ShapeDtype...  38.5 us
    pallas_call x1, Pallas kernels, shards(): pl.pallas_call(copy_kernel, out_shape=[jax.ShapeDtypeStruct(inputs.shape,...  1.97 us

profile of v4, /device:TPU:1, one launch (start us, length us, event | category | flops | bytes accessed | tf_op | source)
XLA Modules:
  0.0 41.1 jit_solution(13276405346671512026)
XLA Ops:
  0.6 38.5 %attention.1 = (bf16[2,24,4,1024]{3,2,1,0:T(4,128)(2,1)}, bf16[2,24,4,1024]{3,2,1,0:T(4,128)(2,1)}) custom-call(bf16[2,24,4,1024]{3,2,1,0:T(4,128)(2,1)} %x_hbm.1, bf16[2,24,4,1024]{3,2,1,0:T(4,128)(2,1)} %go_hbm.1, bf16[1024,1024]{1,0:T(8,128)(2,1)} %wq_hbm.1, bf16[1024,1024]{1,0:T(8,128)(2,1)} %wk_hbm.1, bf16[1024,1024]{1,0:T(8,128)(2,1)} %wv_hbm.1, ...), custom_call_target="tpu_custom_call" | custom-call | tf_op jit(solution)/shard_map/attention/pallas_call | solution.py:506
  39.1 2.0 %copy_out.1 = (bf16[2,24,4,1024]{3,2,1,0:T(4,128)(2,1)}, bf16[2,24,4,1024]{3,2,1,0:T(4,128)(2,1)}) custom-call(bf16[2,24,4,1024]{3,2,1,0:T(4,128)(2,1)} %get-tuple-element.4.a_hbm, bf16[2,24,4,1024]{3,2,1,0:T(4,128)(2,1)} %get-tuple-element.5.b_hbm), custom_call_target="tpu_custom_call" | custom-call | tf_op jit(solution)/shard_map/copy_out/pallas_call | solution.py:528

commit v5 on v4

--- a/solution.py
+++ b/solution.py
@@ -13,7 +13,7 @@
 RW = 7
 PAD = 8
 BR = 8
-NHG = 4
+NHG = 2
 BF = jnp.bfloat16
 F32 = jnp.float32
 
@@ -199,7 +199,7 @@
                 begin += count * size
         return 0
 
-    lax.fori_loop(0, width // tile, step, 0)
+    lax.fori_loop(0, width // tile, step, 0, unroll=2)
 
 
 class Exchange:
@@ -434,10 +434,13 @@
     others = list(range(1, slots // frames))
     ex_x.got_tm([0, 1])
     ex_x.send_rows(others)
+    edges = [(edge, edge), (tokens, edge)]
+    project([to_k(rest, edges), to_v(rest, edges)])
     ex_x.got_tm([2])
     ex_go.send_tm()
     ex_x.got_rows(others)
-    project([to_k(rest, centre + rims), to_v(rest, centre + rims)])
+    left = [(2 * edge, tokens - 2 * edge)] + rims
+    project([to_k(rest, left), to_v(rest, left)])
     inner_blocks(forward)
     ex_go.got_tm([0, 1])
     ex_go.send_rows(others)
@@ -467,7 +470,7 @@
         out_ref[:, :, :, at] = total.astype(BF).reshape(frames, rows, cols, tile)
         return 0
 
-    lax.fori_loop(0, width // tile, out_step, 0)
+    lax.fori_loop(0, width // tile, out_step, 0, unroll=2)
     ex_x.sent()
     ex_go.sent()
     ex_st.sent()

time: 41.2 us -> 43.2 us (1.049)
  Pallas kernels: 40.4 us -> 42.4 us
    pallas_call x1, Pallas kernels: 38.5 us -> 40.4 us  [shards(): pl.pallas_call(functools.partial(kernel, dims), out_shape=[jax.ShapeDtype...]
where the time goes in v5:
time: 43.2 us; the launch traced here: 43 us
  Pallas kernels  42.4 us (98%)
  between operations  0.64 us (1%)
    pallas_call x1, Pallas kernels, shards(): pl.pallas_call(functools.partial(kernel, dims), out_shape=[jax.ShapeDtype...  40.4 us
    pallas_call x1, Pallas kernels, shards(): pl.pallas_call(copy_kernel, out_shape=[jax.ShapeDtypeStruct(inputs.shape,...  1.97 us

profile of v5, /device:TPU:1, one launch (start us, length us, event | category | flops | bytes accessed | tf_op | source)
XLA Modules:
  0.0 43.0 jit_solution(5003603533766402061)
XLA Ops:
  0.6 40.4 %attention.1 = (bf16[2,24,4,1024]{3,2,1,0:T(4,128)(2,1)}, bf16[2,24,4,1024]{3,2,1,0:T(4,128)(2,1)}) custom-call(bf16[2,24,4,1024]{3,2,1,0:T(4,128)(2,1)} %x_hbm.1, bf16[2,24,4,1024]{3,2,1,0:T(4,128)(2,1)} %go_hbm.1, bf16[1024,1024]{1,0:T(8,128)(2,1)} %wq_hbm.1, bf16[1024,1024]{1,0:T(8,128)(2,1)} %wk_hbm.1, bf16[1024,1024]{1,0:T(8,128)(2,1)} %wv_hbm.1, ...), custom_call_target="tpu_custom_call" | custom-call | tf_op jit(solution)/shard_map/attention/pallas_call | solution.py:509
  41.1 2.0 %copy_out.1 = (bf16[2,24,4,1024]{3,2,1,0:T(4,128)(2,1)}, bf16[2,24,4,1024]{3,2,1,0:T(4,128)(2,1)}) custom-call(bf16[2,24,4,1024]{3,2,1,0:T(4,128)(2,1)} %get-tuple-element.4.a_hbm, bf16[2,24,4,1024]{3,2,1,0:T(4,128)(2,1)} %get-tuple-element.5.b_hbm), custom_call_target="tpu_custom_call" | custom-call | tf_op jit(solution)/shard_map/copy_out/pallas_call | solution.py:531

commit v6 on v4

--- a/solution.py
+++ b/solution.py
@@ -336,8 +336,8 @@
 
 def kernel(
     dims, x_hbm, go_hbm, wq_hbm, wk_hbm, wv_hbm, wo_hbm,
-    attended_ref, out_ref,
-    x_ref, go_ref, q_ref, k_ref, v_ref, g_ref, wq_ref, wk_ref, wv_ref, wo_ref,
+    attended_hbm, out_hbm,
+    attended_ref, out_ref, x_ref, go_ref, q_ref, k_ref, v_ref, g_ref, wq_ref, wk_ref, wv_ref, wo_ref,
     mixed_ref, dq_ref, dk_ref, dv_ref, stat_ref, bias_ref, x4_ref, go4_ref, mask_ref, local_sem,
     *sems,
 ):
@@ -434,10 +434,13 @@
     others = list(range(1, slots // frames))
     ex_x.got_tm([0, 1])
     ex_x.send_rows(others)
+    edges = [(edge, edge), (tokens, edge)]
+    project([to_k(rest, edges), to_v(rest, edges)])
     ex_x.got_tm([2])
     ex_go.send_tm()
     ex_x.got_rows(others)
-    project([to_k(rest, centre + rims), to_v(rest, centre + rims)])
+    left = [(2 * edge, tokens - 2 * edge)] + rims
+    project([to_k(rest, left), to_v(rest, left)])
     inner_blocks(forward)
     ex_go.got_tm([0, 1])
     ex_go.send_rows(others)
@@ -453,11 +456,17 @@
     ])
     ex_st.got_tm([0, 1])
     ex_st.send_rows(others)
+    attended_copy = pltpu.make_async_copy(attended_ref, attended_hbm, local_sem.at[6])
+    attended_copy.start()
     ex_st.got_tm([2])
     inner_blocks(backward)
     ex_st.got_rows([0] + others)
     outer_blocks(backward)
     tile = 256
+
+    def out_copy(i):
+        at = (slice(None), slice(None), slice(None), pl.ds(pl.multiple_of(i * tile, tile), tile))
+        return pltpu.make_async_copy(out_ref.at[at], out_hbm.at[at], local_sem.at[7 + i])
 
     def out_step(i, _):
         at = pl.ds(pl.multiple_of(i * tile, tile), tile)
@@ -465,12 +474,16 @@
         total += dot_nt(dk_ref[...].reshape(frames * tokens, width), wk_ref[at, :])
         total += dot_nt(dv_ref[...].reshape(frames * tokens, width), wv_ref[at, :])
         out_ref[:, :, :, at] = total.astype(BF).reshape(frames, rows, cols, tile)
+        out_copy(i).start()
         return 0
 
     lax.fori_loop(0, width // tile, out_step, 0)
     ex_x.sent()
     ex_go.sent()
     ex_st.sent()
+    attended_copy.wait()
+    for i in range(width // tile):
+        out_copy(i).wait()
 
 
 def copy_kernel(a_hbm, b_hbm, a_out, b_out, held_ref, in_sem, out_sem):
@@ -499,7 +512,6 @@
     wide = tokens + 2 * PAD * cols
     keys = slots * (BR + 2 * PAD) * cols
     mine = frames * BR * cols
-    vmem = pl.BlockSpec(memory_space=pltpu.VMEM)
     hbm = pl.BlockSpec(memory_space=pl.ANY)
     links = 3 * (groups - 1)
     sems = [pltpu.SemaphoreType.DMA((links,))] * 2 + [pltpu.SemaphoreType.DMA((2 * groups,))] * 2
@@ -507,8 +519,9 @@
         functools.partial(kernel, dims),
         out_shape=[jax.ShapeDtypeStruct(inputs.shape, BF)] * 2,
         in_specs=[hbm] * 6,
-        out_specs=[vmem] * 2,
-        scratch_shapes=[pltpu.VMEM((slots, wide, width), BF)] * 6
+        out_specs=[hbm] * 2,
+        scratch_shapes=[pltpu.VMEM(inputs.shape, BF)] * 2
+        + [pltpu.VMEM((slots, wide, width), BF)] * 6
         + [pltpu.VMEM((width, width), BF)] * 4
         + [pltpu.VMEM((frames, tokens, width), BF)] * 4
         + [
@@ -517,7 +530,7 @@
             pltpu.VMEM(inputs.shape, BF),
             pltpu.VMEM(inputs.shape, BF),
             pltpu.VMEM((NHG, mine, NHG * HD), BF),
-            pltpu.SemaphoreType.DMA((6,)),
+            pltpu.SemaphoreType.DMA((7 + width // 256,)),
         ]
         + sems * 3,
         compiler_params=pltpu.CompilerParams(

time: 41.2 us -> 41 us (level)
  no operation moved by 1% of the time
where the time goes in v6:
time: 41 us; the launch traced here: 40.8 us
  Pallas kernels  40.2 us (98%)
  between operations  0.64 us (2%)
    pallas_call x1, Pallas kernels, shards(): pl.pallas_call(functools.partial(kernel, dims), out_shape=[jax.ShapeDtype...  38.2 us
    pallas_call x1, Pallas kernels, shards(): pl.pallas_call(copy_kernel, out_shape=[jax.ShapeDtypeStruct(inputs.shape,...  1.97 us

profile of v6, /device:TPU:1, one launch (start us, length us, event | category | flops | bytes accessed | tf_op | source)
XLA Modules:
  0.0 40.8 jit_solution(18104472437276190889)
XLA Ops:
  0.6 38.2 %attention.1 = (bf16[2,24,4,1024]{3,2,1,0:T(4,128)(2,1)}, bf16[2,24,4,1024]{3,2,1,0:T(4,128)(2,1)}) custom-call(bf16[2,24,4,1024]{3,2,1,0:T(4,128)(2,1)} %x_hbm.1, bf16[2,24,4,1024]{3,2,1,0:T(4,128)(2,1)} %go_hbm.1, bf16[1024,1024]{1,0:T(8,128)(2,1)} %wq_hbm.1, bf16[1024,1024]{1,0:T(8,128)(2,1)} %wk_hbm.1, bf16[1024,1024]{1,0:T(8,128)(2,1)} %wv_hbm.1, ...), custom_call_target="tpu_custom_call" | custom-call | tf_op jit(solution)/shard_map/attention/pallas_call | solution.py:518
  38.9 2.0 %copy_out.1 = (bf16[2,24,4,1024]{3,2,1,0:T(4,128)(2,1)}, bf16[2,24,4,1024]{3,2,1,0:T(4,128)(2,1)}) custom-call(bf16[2,24,4,1024]{3,2,1,0:T(4,128)(2,1)} %get-tuple-element.4.a_hbm, bf16[2,24,4,1024]{3,2,1,0:T(4,128)(2,1)} %get-tuple-element.5.b_hbm), custom_call_target="tpu_custom_call" | custom-call | tf_op jit(solution)/shard_map/copy_out/pallas_call | solution.py:541
